TPU v7x, 32 devices: a whole 2x2x4 slice. The times are simulated.
32 devices in a mesh: tile: 8 (over z, y), flow: 4 (over x, core).
Axes of the slice: x: 2, y: 2, z: 4, core: 2. Of those that a mesh axis runs over, the one named last changes fastest.
Arguments:
- density: float32 [64, 1024, 512], P(None, 'tile', 'flow'), may hold values from 0 to 2
- habitat_class: int32 [1024, 512], P('tile', 'flow'), may hold values from 0 to 15
- suitability: float32 [16], replicated, may hold values from 0.2 to 1
- dispersal_draw: bfloat16 [64, 1024, 512], P(None, 'tile', 'flow'), may hold values from 0 to 1
- threshold: float32 [1024, 512], P('tile', 'flow'), may hold values from 0.2 to 0.8
- hub_row: int32 [4, 128], P('flow', 'tile'), may hold values from 0 to 127
- dest_tile: int32 [4, 128, 1], P('flow', 'tile'), may hold values from 0 to 7; in each aligned block of 16 rows (0 to 15, 16 to 31, ..., all dimensions but the last counted through in order) at most 4 rows name the same one
- dest_row: int32 [4, 128], P('flow', 'tile'), may hold values from 0 to 127
- county_id: int32 [4, 128], P('flow', 'tile'), may hold values from 0 to 15
- jump_share: float32 [4, 128], P('flow', 'tile'), may hold values from 0.1 to 0.4
- flow_tiles: bfloat16 [16, 128, 128], P('flow'), may hold values from 0 to 0.019897461
- flow_scale: bfloat16 [16], P('flow'), may hold values from 0.5 to 2
Outputs:
- density_next: float32 [64, 1024, 512], P(None, 'tile', 'flow')
Inputs may be any that keep to these rules, and one draw needn't show every extreme that they name: `dest_tile`: among the 16 hubs of one device, at most 4 reach the same band, and in every draw some band gets exactly 4 of them.
All inputs are finite; a program needn't handle non-finite values.
Results may differ from a plain program's by a relative error of at most 0.00043.
Values may be sent and summed in bfloat16 or wider, within the bound.
No kernel may reach another device: no remote copies, remote signals or barrier semaphores. Data moves between devices by JAX's collectives and lax.ppermute only.
A program may use at most 64 MiB of HBM per device.

v0:
```python
import jax
import jax.numpy as jnp
from jax import lax
from jax.sharding import PartitionSpec as P

STEPS = 2
CAP = 4


KAPPA = 0.24
SHARPNESS = 8.0


def with_halo(cells, sides, width):
    for axis, dim in sides:
        count = lax.axis_size(axis)
        ends = count - 1
        head = lax.slice_in_dim(cells, 0, width, axis=dim)
        tail = lax.slice_in_dim(cells, cells.shape[dim] - width, cells.shape[dim], axis=dim)
        cells = jnp.concatenate(
            [
                lax.ppermute(tail, axis, [(i, (i + 1) % count) for i in range(ends)]),
                cells,
                lax.ppermute(head, axis, [((i + 1) % count, i) for i in range(ends)]),
            ],
            axis=dim,
        )
    return cells


def relax(padded, centre_weight):
    centre = padded[:, 1:-1, 1:-1]
    beside_all = (
        padded[:, 2:, 1:-1] + padded[:, :-2, 1:-1] + padded[:, 1:-1, 2:] + padded[:, 1:-1, :-2]
    )
    return centre + KAPPA * centre_weight * (beside_all - 4.0 * centre)


def local(
    density,
    habitat_class,
    suitability,
    dispersal_draw,
    threshold,
    hub_row,
    dest_tile,
    dest_row,
    county_id,
    jump_share,
    flow_tiles,
    flow_scale,
):
    members, rows_dev, cols_dev = density.shape
    weight = jnp.zeros((rows_dev, cols_dev), jnp.float32)
    for label in range(suitability.shape[0]):
        weight = weight + jnp.where(habitat_class == label, suitability[label], 0.0)
    stacked = jnp.concatenate([density, weight[None]], axis=0)
    field = density
    for step in range(STEPS):
        if step == 0:
            extended = with_halo(stacked, (("tile", 1), ("flow", 2)), 1)
            field = extended[:members]
        else:
            field = with_halo(field, (("tile", 1), ("flow", 2)), 1)
        field = relax(field, weight)
    hubs = hub_row.reshape(-1)
    targets = dest_tile.reshape(-1)
    arrive_rows = dest_row.reshape(-1)
    county = county_id.reshape(-1)
    share = jump_share.reshape(-1)
    count_hubs = hubs.shape[0]
    slots = CAP * lax.axis_size("tile")
    picked = jnp.take(field, hubs, axis=1)
    moved = share[None, :, None] * picked
    anchor = (hubs[:, None] == jnp.arange(rows_dev, dtype=jnp.int32)[None, :]).astype(jnp.float32)
    field = field - jnp.einsum("hr,mhk->mrk", anchor, moved, precision=lax.Precision.HIGHEST)
    outgoing = jnp.moveaxis(moved, 1, 0).astype(jnp.bfloat16)
    order = jnp.arange(count_hubs, dtype=jnp.int32)
    same_band = targets[:, None] == targets[None, :]
    earlier = order[None, :] < order[:, None]
    position = jnp.sum(jnp.logical_and(same_band, earlier).astype(jnp.int32), axis=1)
    place = targets * CAP + position
    placing = jnp.arange(slots, dtype=jnp.int32)[:, None] == place[None, :]
    tiles_all, scales_all = (
        lax.all_gather(flow_tiles, "flow", axis=0, tiled=True),
        lax.all_gather(flow_scale, "flow", axis=0, tiled=True),
    )
    chosen = jnp.take(tiles_all, county, axis=0)
    scales = jnp.take(scales_all, county, axis=0).astype(jnp.float32)
    product = jnp.einsum("hmk,hkj->hmj", outgoing, chosen, preferred_element_type=jnp.float32)
    sent = jnp.einsum(
        "sh,hmk->smk",
        placing.astype(jnp.bfloat16),
        (product * scales[:, None, None]).astype(jnp.bfloat16),
        preferred_element_type=jnp.float32,
    ).astype(jnp.bfloat16)
    row_tags = jnp.sum(jnp.where(placing, (arrive_rows + 1)[None, :], 0), axis=1)
    landed, tags = (
        lax.all_to_all(sent, "tile", split_axis=0, concat_axis=0, tiled=True),
        lax.all_to_all(row_tags, "tile", split_axis=0, concat_axis=0, tiled=True),
    )
    landing = (tags[:, None] - 1 == jnp.arange(rows_dev, dtype=jnp.int32)[None, :]).astype(
        jnp.bfloat16
    )
    field = field + jnp.einsum("sr,smk->mrk", landing, landed, preferred_element_type=jnp.float32)
    grow = jax.nn.sigmoid(SHARPNESS * (dispersal_draw.astype(jnp.float32) - threshold))
    return field * grow


def solution(mesh):
    in_specs = (
        P(None, "tile", "flow"),
        P("tile", "flow"),
        P(),
        P(None, "tile", "flow"),
        P("tile", "flow"),
        P("flow", "tile"),
        P("flow", "tile", None),
        P("flow", "tile"),
        P("flow", "tile"),
        P("flow", "tile"),
        P("flow", None, None),
        P("flow"),
    )
    out_specs = P(None, "tile", "flow")
    return jax.shard_map(local, mesh=mesh, in_specs=in_specs, out_specs=out_specs, check_vma=False)
```

profile of v0, /device:TPU:1, one launch (start us, length us, event | category | flops | bytes accessed | tf_op | source)
XLA Modules:
  0.0 193.9 jit_solution(5498426266046277973)
XLA Ops:
  2.9 5.6 %copy.124 = f32[64,128,128]{1,2,0:T(8,128)} copy(f32[64,128,128]{2,1,0:T(8,128)} %param.12) | data formatting | bytes 8388608 | tf_op args[0]
  8.5 10.2 %broadcast_multiply_fusion = (f32[128,128]{0,1:T(8,128)S(1)}, f32[128,128]{0,1:T(8,128)S(1)}) fusion(f32[]{:T(128)} %bitcast.15, s32[128,128]{0,1:T(8,128)S(1)} %copy.100, f32[]{:T(128)} %bitcast.14, f32[]{:T(128)} %bitcast.13, f32[]{:T(128)} %bitcast.12, f32[]{:T(128)} %bitcast.11, f32[]{:T(128)} %bitcast.10, f32[]{:T(128)} %bitcast.9, f32[]{:T(128)} %bitcast.8, ...), kind=kLoop, calls=%fused_computation.61 | loop fusion | flops 786432 | bytes 196672 | tf_op jit(solution)/shard_map/mul | solution.py:36
  18.7 6.7 %pad_maximum_fusion = (f32[65,1,128]{1,2,0:T(8,128)}, f32[65,1,128]{1,2,0:T(8,128)}) fusion(f32[1,128,128]{1,2,0:T(8,128)S(1)} %bitcast.59, f32[64,128,128]{1,2,0:T(8,128)} %copy.124), kind=kLoop, calls=%fused_computation.3 | loop fusion | flops 16640 | bytes 4326400 | tf_op jit(solution)/shard_map/concatenate | solution.py:57
  25.5 3.0 %copy.117 = f32[65,1,128]{2,1,0:T(1,128)S(1)} copy(f32[65,1,128]{1,2,0:T(8,128)} %get-tuple-element.14) | data formatting | bytes 66560 | tf_op jit(solution)/shard_map/slice | solution.py:18
  29.7 2.9 %copy.119 = f32[65,1,128]{2,1,0:T(1,128)S(1)} copy(f32[65,1,128]{1,2,0:T(8,128)} %get-tuple-element.13) | data formatting | bytes 66560 | tf_op jit(solution)/shard_map/slice | solution.py:19
  32.7 4.6 %collective-permute-start.1 = (f32[65,1,128]{2,1,0:T(1,128)S(1)}, f32[65,1,128]{2,1,0:T(1,128)S(1)}, u32[]{:S(2)}, u32[]{:S(2)}) collective-permute-start(f32[65,1,128]{2,1,0:T(1,128)S(1)} %copy.119), channel_id=1, source_target_pairs={{0,4},{4,8},{8,12},{12,16},{16,20},{20,24},{24,28},{1,5},{5,9},{9,... | collective-permute-start | bytes 99848 | tf_op jit(solution)/shard_map/ppermute | solution.py:22
  38.3 5.7 %all-to-all-start.1 = ((s32[8,4,1]{1,2,0:T(1,128)}), s32[8,4,1]{1,2,0:T(1,128)S(1)}, u32[]{:S(2)}, u32[]{:S(2)}) async-start(s32[8,4,1]{1,2,0:T(1,128)} %bitcast.32), calls=%async_computation.1 | async-start | bytes 8192 | tf_op jit(solution)/shard_map/all_to_all | solution.py:100
  45.6 6.5 %all-reduce = bf16[16]{0:T(256)(128)(2,1)S(1)} all-reduce(bf16[16]{0:T(256)(128)(2,1)S(1)} %dynamic-update-slice), channel_id=1, replica_groups=mesh['tile'=8,'flow'=4] {'flow'}, use_global_device_ids=true, to_apply=%add | all-reduce | flops 16 | bytes 64
  60.3 2.9 %collective-permute-start.2 = (f32[65,130,1]{1,2,0:T(1,128)S(1)}, f32[65,130,1]{1,2,0:T(1,128)S(1)}, u32[]{:S(2)}, u32[]{:S(2)}) collective-permute-start(f32[65,130,1]{1,2,0:T(1,128)S(1)} %get-tuple-element.9), channel_id=1, source_target_pairs={{1,0},{2,1},{3,2},{5,4},{6,5},{7,6},{9,8},{10,9},{11,10},{13,12},{... | collective-permute-start | bytes 101408 | tf_op jit(solution)/shard_map/ppermute | solution.py:24
  63.2 3.1 %collective-permute-start.3 = (f32[65,130,1]{1,2,0:T(1,128)S(1)}, f32[65,130,1]{1,2,0:T(1,128)S(1)}, u32[]{:S(2)}, u32[]{:S(2)}) collective-permute-start(f32[65,130,1]{1,2,0:T(1,128)S(1)} %get-tuple-element.10), channel_id=1, source_target_pairs={{0,1},{1,2},{2,3},{4,5},{5,6},{6,7},{8,9},{9,10},{10,11},{12,13},{... | collective-permute-start | bytes 101408 | tf_op jit(solution)/shard_map/ppermute | solution.py:22
  67.5 23.0 %fusion.9 = f32[64,128,128]{1,2,0:T(8,128)S(1)} fusion(f32[64,128,128]{1,2,0:T(8,128)} %copy.124, f32[65,130,1]{1,2,0:T(1,128)S(1)} %collective-permute-done.3, f32[65,1,128]{1,2,0:T(8,128)} %copy.118, f32[65,1,128]{1,2,0:T(8,128)} %copy.120, f32[1,128,128]{1,2,0:T(8,128)S(1)} %bitcast.61, f32[65,130,1]{1,2,0:T(1,128)S(1)} %collective-permute-done.2, ...), kind=kLoop, calls=%fused_computation.23 | loop fusion | flops 19922944 | bytes 8653840 | tf_op jit(solution)/shard_map/add | solution.py:36
  90.4 4.8 %fusion.36 = (f32[64,1,128]{1,2,0:T(8,128)}, f32[64,1,128]{1,2,0:T(8,128)}) fusion(f32[64,128,128]{1,2,0:T(8,128)S(1)} %fusion.9), kind=kLoop, calls=%fused_computation.90 | loop fusion | bytes 131072 | tf_op jit(solution)/shard_map/slice | solution.py:19
  102.3 4.2 %collective-permute-start.5 = (f32[64,1,128]{2,0,1:T(8,128)S(1)}, f32[64,1,128]{2,0,1:T(8,128)S(1)}, u32[]{:S(2)}, u32[]{:S(2)}) collective-permute-start(f32[64,1,128]{2,0,1:T(8,128)S(1)} %copy.127), channel_id=1, source_target_pairs={{0,4},{4,8},{8,12},{12,16},{16,20},{20,24},{24,28},{1,5},{5,9},{9,... | collective-permute-start | bytes 98312 | tf_op jit(solution)/shard_map/ppermute | solution.py:22
  106.5 8.6 %all_gather.6 = bf16[16,128,128]{2,1,0:T(8,128)(2,1)S(1)} all-gather(bf16[4,128,128]{2,1,0:T(8,128)(2,1)S(1)} %copy-done.3), channel_id=1, replica_groups=mesh['tile'=8,'flow'=4] {'flow'}, dimensions={0}, use_global_device_ids=true | all-gather | bytes 655360 | tf_op jit(solution)/shard_map/all_gather | solution.py:85
  124.3 3.7 %collective-permute-start.7 = (f32[64,130,1]{1,2,0:T(1,128)S(1)}, f32[64,130,1]{1,2,0:T(1,128)S(1)}, u32[]{:S(2)}, u32[]{:S(2)}) collective-permute-start(f32[64,130,1]{1,2,0:T(1,128)S(1)} %get-tuple-element.12), channel_id=1, source_target_pairs={{0,1},{1,2},{2,3},{4,5},{5,6},{6,7},{8,9},{9,10},{10,11},{12,13},{... | collective-permute-start | bytes 99848 | tf_op jit(solution)/shard_map/ppermute | solution.py:22
  129.1 20.2 %fusion.3 = f32[64,128,128]{1,2,0:T(8,128)} fusion(f32[64,128,128]{1,2,0:T(8,128)} %copy-done, f32[64,130,1]{1,2,0:T(1,128)S(1)} %collective-permute-done.7, f32[64,1,128]{1,2,0:T(8,128)} %copy.126, f32[64,1,128]{1,2,0:T(8,128)} %copy.128, f32[64,130,1]{1,2,0:T(1,128)S(1)} %collective-permute-done.6, f32[128,128]{0,1:T(8,128)S(1)} %get-tuple-element.7), kind=kLoop, calls=%fused_computation.9 | loop fusion | flops 15728640 | bytes 8586240 | tf_op jit(solution)/shard_map/add | solution.py:36
  149.3 5.3 %copy.131 = f32[64,128,128]{2,0,1:T(8,128)} copy(f32[64,128,128]{1,2,0:T(8,128)} %fusion.3) | data formatting | bytes 8388608 | tf_op jit(solution)/shard_map/add | solution.py:36
  154.7 3.7 %gather_fusion = f32[16,64,128]{2,1,0:T(8,128)} fusion(f32[64,128,128]{2,0,1:T(8,128)} %copy.131, s32[1024]{0:T(1024)S(1)} %pad_clamp_fusion.1), kind=kCustom, calls=%fused_computation | custom fusion | bytes 1048640 | tf_op jit(solution)/shard_map/jit(_take)/gather | solution.py:73
  161.3 5.7 %all-to-all-start = ((bf16[32,64,128]{2,1,0:T(8,128)(2,1)}), bf16[32,64,128]{2,1,0:T(8,128)(2,1)S(1)}, u32[]{:S(2)}, u32[]{:S(2)}) async-start(bf16[32,64,128]{2,1,0:T(8,128)(2,1)} %copy.134), calls=%async_computation | async-start | bytes 1048576 | tf_op jit(solution)/shard_map/all_to_all | solution.py:99
  167.0 2.9 %copy.137 = bf16[64,128,128]{1,2,0:T(8,128)(2,1)} copy(bf16[64,128,128]{2,1,0:T(8,128)(2,1)S(1)} %copy-done.1) | data formatting | bytes 4194304 | tf_op args[3]
  170.1 5.0 %fusion.15 = f32[64,128,128]{2,1,0:T(8,128)} fusion(f32[64,16,128]{2,0,1:T(8,128)S(1)} %multiply_bitcast_fusion, s32[16]{0:T(128)S(1)} %bitcast.63), kind=kOutput, calls=%fused_computation.44 | convolution fusion | flops 201328640 | bytes 4718656 | tf_op jit(solution)/shard_map/hr,mhk->mrk/dot_general | solution.py:76
  175.1 5.9 %all-to-all-done = bf16[32,64,128]{2,1,0:T(8,128)(2,1)S(1)} async-done(((bf16[32,64,128]{2,1,0:T(8,128)(2,1)}), bf16[32,64,128]{2,1,0:T(8,128)(2,1)S(1)}, u32[]{:S(2)}, u32[]{:S(2)}) %all-to-all-start) | async-done | bytes 524320 | tf_op jit(solution)/shard_map/all_to_all | solution.py:99
  181.0 7.2 %fusion.12 = f32[64,128,128]{1,2,0:T(8,128)} fusion(f32[64,128,128]{1,2,0:T(8,128)} %fusion.3, f32[64,128,128]{2,1,0:T(8,128)} %fusion.15, bf16[64,128,128]{1,2,0:T(8,128)(2,1)S(1)} %copy-done.2, f32[128,128]{0,1:T(8,128)S(1)} %copy.138, bf16[32,64,128]{2,1,0:T(8,128)(2,1)S(1)} %all-to-all-done, s32[32]{0:T(128)S(1)} %sub.27), kind=kOutput, calls=%fused_computation.38 | convolution fusion | flops 76550144 | bytes 15270016 | tf_op jit(solution)/shard_map/sr,smk->mrk/dot_general | solution.py:105
  188.3 5.6 %copy.139 = f32[64,128,128]{2,1,0:T(8,128)} copy(f32[64,128,128]{1,2,0:T(8,128)} %fusion.12) | data formatting | bytes 8388608 | tf_op jit(solution)/shard_map/mul | solution.py:107
  (69 shorter events, 35.7 us)
Async XLA Ops:
  25.4 11.9 %copy-start.8 = (s32[1,16,1]{1,2,0:T(1,128)S(1)}, s32[1,16,1]{1,2,0:T(1,128)}, u32[]{:S(2)}) copy-start(s32[1,16,1]{1,2,0:T(1,128)} %param.18) | copy-start | bytes 196
  25.4 12.1 %copy-start.9 = (s32[1,16]{1,0:T(1,128)S(1)}, s32[1,16]{1,0:T(1,128)}, u32[]{:S(2)}) copy-start(s32[1,16]{1,0:T(1,128)} %param.19) | copy-start | bytes 196
  25.4 18.5 %copy-start.7 = (s32[1,16]{1,0:T(1,128)S(1)}, s32[1,16]{1,0:T(1,128)}, u32[]{:S(2)}) copy-start(s32[1,16]{1,0:T(1,128)} %param.20) | copy-start | bytes 196
  25.4 18.5 %copy-start.11 = (u32[32]{0:T(128)S(1)}, u32[32]{0:T(128)}, u32[]{:S(2)}) copy-start(u32[32]{0:T(128)} %constant.96) | copy-start | bytes 388
  25.4 19.9 %copy-start.10 = (bf16[4]{0:T(256)(128)(2,1)S(1)}, bf16[4]{0:T(256)(128)(2,1)}, u32[]{:S(2)}) copy-start(bf16[4]{0:T(256)(128)(2,1)} %param.23) | copy-start | bytes 28
  25.4 27.4 %copy-start.6 = (s32[1,16]{1,0:T(1,128)S(1)}, s32[1,16]{1,0:T(1,128)}, u32[]{:S(2)}) copy-start(s32[1,16]{1,0:T(1,128)} %param.17) | copy-start | bytes 196
  28.4 24.4 %collective-permute-start = (f32[65,1,128]{2,1,0:T(1,128)S(1)}, f32[65,1,128]{2,1,0:T(1,128)S(1)}, u32[]{:S(2)}, u32[]{:S(2)}) collective-permute-start(f32[65,1,128]{2,1,0:T(1,128)S(1)} %copy.117), channel_id=1, source_target_pairs={{4,0},{8,4},{12,8},{16,12},{20,16},{24,20},{28,24},{5,1},{9,5},{13... | collective-permute-start | bytes 99848 | tf_op jit(solution)/shard_map/ppermute | solution.py:24
  32.7 22.9 %collective-permute-start.1 = (f32[65,1,128]{2,1,0:T(1,128)S(1)}, f32[65,1,128]{2,1,0:T(1,128)S(1)}, u32[]{:S(2)}, u32[]{:S(2)}) collective-permute-start(f32[65,1,128]{2,1,0:T(1,128)S(1)} %copy.119), channel_id=1, source_target_pairs={{0,4},{4,8},{8,12},{12,16},{16,20},{20,24},{24,28},{1,5},{5,9},{9,... | collective-permute-start | bytes 99848 | tf_op jit(solution)/shard_map/ppermute | solution.py:22
  38.3 123.1 %all-to-all-start.1 = ((s32[8,4,1]{1,2,0:T(1,128)}), s32[8,4,1]{1,2,0:T(1,128)S(1)}, u32[]{:S(2)}, u32[]{:S(2)}) async-start(s32[8,4,1]{1,2,0:T(1,128)} %bitcast.32), calls=%async_computation.1 | async-start | bytes 8192 | tf_op jit(solution)/shard_map/all_to_all | solution.py:100
  60.3 6.1 %collective-permute-start.2 = (f32[65,130,1]{1,2,0:T(1,128)S(1)}, f32[65,130,1]{1,2,0:T(1,128)S(1)}, u32[]{:S(2)}, u32[]{:S(2)}) collective-permute-start(f32[65,130,1]{1,2,0:T(1,128)S(1)} %get-tuple-element.9), channel_id=1, source_target_pairs={{1,0},{2,1},{3,2},{5,4},{6,5},{7,6},{9,8},{10,9},{11,10},{13,12},{... | collective-permute-start | bytes 101408 | tf_op jit(solution)/shard_map/ppermute | solution.py:24
  63.2 4.3 %collective-permute-start.3 = (f32[65,130,1]{1,2,0:T(1,128)S(1)}, f32[65,130,1]{1,2,0:T(1,128)S(1)}, u32[]{:S(2)}, u32[]{:S(2)}) collective-permute-start(f32[65,130,1]{1,2,0:T(1,128)S(1)} %get-tuple-element.10), channel_id=1, source_target_pairs={{0,1},{1,2},{2,3},{4,5},{5,6},{6,7},{8,9},{9,10},{10,11},{12,13},{... | collective-permute-start | bytes 101408 | tf_op jit(solution)/shard_map/ppermute | solution.py:22
  90.4 4.8 %copy-start = (f32[64,128,128]{1,2,0:T(8,128)}, f32[64,128,128]{1,2,0:T(8,128)S(1)}, u32[]{:S(2)}) copy-start(f32[64,128,128]{1,2,0:T(8,128)S(1)} %fusion.9) | copy-start | bytes 12582916
  95.2 11.2 %copy-start.3 = (bf16[4,128,128]{2,1,0:T(8,128)(2,1)S(1)}, bf16[4,128,128]{2,1,0:T(8,128)(2,1)}, u32[]{:S(2)}) copy-start(bf16[4,128,128]{2,1,0:T(8,128)(2,1)} %param.22) | copy-start | bytes 393220
  98.1 17.0 %collective-permute-start.4 = (f32[64,1,128]{2,0,1:T(8,128)S(1)}, f32[64,1,128]{2,0,1:T(8,128)S(1)}, u32[]{:S(2)}, u32[]{:S(2)}) collective-permute-start(f32[64,1,128]{2,0,1:T(8,128)S(1)} %copy.125), channel_id=1, source_target_pairs={{4,0},{8,4},{12,8},{16,12},{20,16},{24,20},{28,24},{5,1},{9,5},{13... | collective-permute-start | bytes 98312 | tf_op jit(solution)/shard_map/ppermute | solution.py:24
  102.3 15.5 %collective-permute-start.5 = (f32[64,1,128]{2,0,1:T(8,128)S(1)}, f32[64,1,128]{2,0,1:T(8,128)S(1)}, u32[]{:S(2)}, u32[]{:S(2)}) collective-permute-start(f32[64,1,128]{2,0,1:T(8,128)S(1)} %copy.127), channel_id=1, source_target_pairs={{0,4},{4,8},{8,12},{12,16},{16,20},{20,24},{24,28},{1,5},{5,9},{9,... | collective-permute-start | bytes 98312 | tf_op jit(solution)/shard_map/ppermute | solution.py:22
  122.2 6.5 %collective-permute-start.6 = (f32[64,130,1]{1,2,0:T(1,128)S(1)}, f32[64,130,1]{1,2,0:T(1,128)S(1)}, u32[]{:S(2)}, u32[]{:S(2)}) collective-permute-start(f32[64,130,1]{1,2,0:T(1,128)S(1)} %get-tuple-element.11), channel_id=1, source_target_pairs={{1,0},{2,1},{3,2},{5,4},{6,5},{7,6},{9,8},{10,9},{11,10},{13,12},{... | collective-permute-start | bytes 99848 | tf_op jit(solution)/shard_map/ppermute | solution.py:24
  124.3 4.8 %collective-permute-start.7 = (f32[64,130,1]{1,2,0:T(1,128)S(1)}, f32[64,130,1]{1,2,0:T(1,128)S(1)}, u32[]{:S(2)}, u32[]{:S(2)}) collective-permute-start(f32[64,130,1]{1,2,0:T(1,128)S(1)} %get-tuple-element.12), channel_id=1, source_target_pairs={{0,1},{1,2},{2,3},{4,5},{5,6},{6,7},{8,9},{9,10},{10,11},{12,13},{... | collective-permute-start | bytes 99848 | tf_op jit(solution)/shard_map/ppermute | solution.py:22
  149.3 9.1 %copy-start.5 = (f32[1,16]{1,0:T(1,128)S(1)}, f32[1,16]{1,0:T(1,128)}, u32[]{:S(2)}) copy-start(f32[1,16]{1,0:T(1,128)} %param.21) | copy-start | bytes 196
  154.7 12.3 %copy-start.1 = (bf16[64,128,128]{2,1,0:T(8,128)(2,1)S(1)}, bf16[64,128,128]{2,1,0:T(8,128)(2,1)}, u32[]{:S(2)}) copy-start(bf16[64,128,128]{2,1,0:T(8,128)(2,1)} %param.15) | copy-start | bytes 6291460
  159.6 10.4 %copy-start.4 = (f32[128,128]{1,0:T(8,128)S(1)}, f32[128,128]{1,0:T(8,128)}, u32[]{:S(2)}) copy-start(f32[128,128]{1,0:T(8,128)} %param.16) | copy-start | bytes 196612
  161.3 19.7 %all-to-all-start = ((bf16[32,64,128]{2,1,0:T(8,128)(2,1)}), bf16[32,64,128]{2,1,0:T(8,128)(2,1)S(1)}, u32[]{:S(2)}, u32[]{:S(2)}) async-start(bf16[32,64,128]{2,1,0:T(8,128)(2,1)} %copy.134), calls=%async_computation | async-start | bytes 1048576 | tf_op jit(solution)/shard_map/all_to_all | solution.py:99
  169.9 11.1 %copy-start.2 = (bf16[64,128,128]{1,2,0:T(8,128)(2,1)S(1)}, bf16[64,128,128]{1,2,0:T(8,128)(2,1)}, u32[]{:S(2)}) copy-start(bf16[64,128,128]{1,2,0:T(8,128)(2,1)} %copy.137) | copy-start | bytes 6291460
where the time goes:
time: 195 us; the launch traced here: 194 us
  other arithmetic  65.2 us (33%)
  local copies, waits for them, and re-layouts  57.5 us (29%)
  starting transfers between devices  34.5 us (18%)
  blocking collectives  15.2 us (8%)
  matrix products  13 us (7%)
  waiting for transfers between devices  7.44 us (4%)
    add x2, other arithmetic, relax(): return centre + KAPPA * centre_weight * (beside_all - 4.0 * centre)  43.1 us
    ppermute x4, starting transfers between devices, with_halo(): lax.ppermute(tail, axis, [(i, (i + 1) % count) for i in range(ends)])  15.6 us
    slice x3, local copies, waits for them, and re-layouts, with_halo(): lax.slice_in_dim(cells, cells.shape[dim] - width, cells.shape[dim], axis=...  10.6 us
    unnamed x31, local copies, waits for them, and re-layouts  10.5 us
    mul x1, other arithmetic, relax(): return centre + KAPPA * centre_weight * (beside_all - 4.0 * centre)  10.2 us
    all_gather x1, blocking collectives, local(): lax.all_gather(flow_tiles, 'flow', axis=0, tiled=True)  8.62 us
    ppermute x4, starting transfers between devices, with_halo(): lax.ppermute(head, axis, [((i + 1) % count, i) for i in range(ends)])  7.59 us
    dot_general x1, matrix products, local(): jnp.einsum('sr,smk->mrk', landing, landed, preferred_element_type=jnp.flo...  7.25 us
  transfers between devices with their start and end apart: 10, of which 3 were waited for; matrix products, arithmetic and copies ran while one was open for 48% of the time, Pallas kernels for 0%

commit v1 on v0

v1 whole, which is shorter than its diff:
```python
import jax
import jax.numpy as jnp
from jax import lax
from jax.experimental import pallas as pl
from jax.experimental.pallas import tpu as pltpu
from jax.sharding import PartitionSpec as P

CAP = 4
KAPPA = 0.24
SHARPNESS = 8.0
TAIL = 8
TAGS = 16
CHUNK = 16
UNROLL = 4
STEP = 16
GROW = 16
MIB = 1024 * 1024
F32 = jnp.float32
BF16 = jnp.bfloat16


def lanes(shape):
    return lax.broadcasted_iota(jnp.int32, shape, 1)


def sublanes(shape):
    return lax.broadcasted_iota(jnp.int32, shape, 0)


def edges_kernel(
    place, density, habitat, suit, tiles, scale,
    cols_a, cols_b, rows_a, rows_b, own, weight_out, tiles_out, turned,
    acc_e, acc_o, label_v, suit_v, scale_v, row_sems, sems,
):
    rows, members, cols = turned.shape
    half = rows // 2
    chunk = CHUNK
    t_even = place[0] == 0
    f_even = place[1] == 0
    depth = tiles.shape[1]
    small = [
        pltpu.make_async_copy(suit, suit_v, sems.at[0]),
        pltpu.make_async_copy(habitat, label_v, sems.at[1]),
        pltpu.make_async_copy(scale, scale_v, sems.at[2]),
        pltpu.make_async_copy(tiles, tiles_out.at[:, :depth, :], sems.at[3]),
    ]
    for copy in small:
        copy.start()

    def fetch(i, carry):
        for k in range(8):
            r = i * 8 + k
            pltpu.make_async_copy(density.at[:, r, :], turned.at[r], row_sems.at[i * 8 // chunk]).start()
        return carry

    lax.fori_loop(0, rows // 8, fetch, 0)
    for copy in small:
        copy.wait()

    shape = (rows, cols)
    label = label_v[...]
    weight = jnp.zeros(shape, F32)
    for c in range(suit_v.shape[0]):
        weight = jnp.where(label == c, suit_v[c], weight)
    weight_out[...] = weight
    pair_lane = lanes((half, cols)) // 2 == sublanes((half, cols))

    def spread(column):
        return jnp.sum(jnp.where(pair_lane, column, 0.0), axis=0, keepdims=True)

    row8 = sublanes((TAIL, cols))

    def side_weight(column):
        return jnp.where(row8 == 0, spread(column[:half]), spread(column[half:]))

    w_right = side_weight(weight[:, cols - 1:])
    w_left = side_weight(weight[:, :1])
    cols_a[2 * members:, :] = jnp.where(f_even, w_right, w_left)
    cols_b[2 * members:, :] = jnp.where(f_even, w_left, w_right)
    w_top = jnp.broadcast_to(weight[:1, :], (TAIL, cols))
    w_bottom = jnp.broadcast_to(weight[rows - 1:, :], (TAIL, cols))
    rows_a[2 * members:, :] = jnp.where(t_even, w_bottom, w_top)
    rows_b[2 * members:, :] = jnp.where(t_even, w_top, w_bottom)
    for c in range(tiles.shape[0]):
        value = scale_v[:, c:c + 1].astype(F32)
        tiles_out[c, depth:, :] = jnp.broadcast_to(value, (TAGS, cols)).astype(BF16)

    quad = lanes((8, cols)) // 4

    def pack(i, carry):
        ready = turned.at[pl.ds(i * chunk, chunk)]
        pltpu.make_async_copy(ready, ready, row_sems.at[i]).wait()
        part = i // (half // chunk)
        first = (i - part * (half // chunk)) * (chunk // 2)
        for g in range(members // 8):
            to = pl.ds(pl.multiple_of(part * members + 8 * g, 8), 8)
            even, odd = acc_e[to, :], acc_o[to, :]
            for j in range(chunk // 2):
                r = i * chunk + 2 * j
                q = first + j
                shift = 4 * q + 2
                hit = quad == q
                even = jnp.where(hit, pltpu.roll(turned[r, 8 * g:8 * g + 8, :], shift, 1), even)
                odd = jnp.where(hit, pltpu.roll(turned[r + 1, 8 * g:8 * g + 8, :], shift, 1), odd)
            acc_e[to, :] = even
            acc_o[to, :] = odd
        return carry

    lax.fori_loop(0, rows // chunk, pack, 0)

    wide = (2 * members, cols)
    low = lanes(wide) % 4 < 2
    even, odd = acc_e[...], acc_o[...]
    right = jnp.where(low, even, pltpu.roll(odd, 2, 1))
    left = jnp.where(low, pltpu.roll(even, cols - 2, 1), odd)
    own[...] = jnp.where(lanes(wide) % 2 == 0, pltpu.roll(right, cols - 1, 1), pltpu.roll(left, 1, 1))
    cols_a[:2 * members, :] = jnp.where(f_even, right, left)
    cols_b[:2 * members, :] = jnp.where(f_even, left, right)
    for k in range(2):
        to = pl.ds(k * members, members)
        rows_a[to, :] = turned[jnp.where(t_even, rows - 2, 0) + k]
        rows_b[to, :] = turned[jnp.where(t_even, 0, rows - 2) + k]


def corners_kernel(place, rows_a, rows_b, got_a, got_b, out_a, out_b):
    cols = got_a.shape[1]
    members = (got_a.shape[0] - TAIL) // 2
    t_even = place[0] == 0
    f_even = place[1] == 0
    side = (members, cols)
    swap = (lanes(side) % 2 == 1) == f_even
    top = jnp.where(swap, got_b[:members, :], got_a[:members, :])
    bottom = jnp.where(swap, got_b[members:2 * members, :], got_a[members:2 * members, :])

    def to_row(pair, first):
        east = jnp.where(lanes(side) == 2 * sublanes(side), pair[:, first:first + 1], 0.0)
        west = jnp.where(lanes(side) == 2 * sublanes(side) + 1, pair[:, first + 1:first + 2], 0.0)
        return jnp.sum(east + west, axis=0, keepdims=True)

    top_row = to_row(top, 0)
    bottom_row = to_row(bottom, cols - 2)
    out_a[...] = rows_a[...]
    out_b[...] = rows_b[...]
    at = 2 * members + 1
    out_a[at:at + 1, :] = jnp.where(t_even, bottom_row, top_row)
    out_b[at:at + 1, :] = jnp.where(t_even, top_row, bottom_row)


def hubs_kernel(
    place, hub_row, dest_tile, dest_row, county, share,
    turned, weight, own, cols_a, cols_b, rows_a, rows_b,
    sent, near, halo1, beside, coef, strips, counts,
):
    rows, members, cols = turned.shape
    bands = counts.shape[0]
    t_even = place[0] == 0
    f_even = place[1] == 0
    side = (members, cols)
    lane = lanes(side)
    even_lane = lane % 2 == 0

    tail_n = jnp.where(t_even, rows_b[2 * members:, :], rows_a[2 * members:, :])
    tail_s = jnp.where(t_even, rows_a[2 * members:, :], rows_b[2 * members:, :])
    for k in range(2):
        at = slice(k * members, (k + 1) * members)
        strips[k] = jnp.where(t_even, rows_b[at, :], rows_a[at, :])
        strips[2 + k] = jnp.where(t_even, rows_a[at, :], rows_b[at, :])
    coef[0:8, :] = KAPPA * tail_n
    coef[8:8 + rows, :] = KAPPA * weight[...]
    coef[8 + rows:, :] = KAPPA * tail_s

    def corner(tail):
        row = jnp.broadcast_to(tail[1:2, :], side)
        east = jnp.sum(jnp.where(lane == 2 * sublanes(side), row, 0.0), axis=1, keepdims=True)
        west = jnp.sum(jnp.where(lane == 2 * sublanes(side) + 1, row, 0.0), axis=1, keepdims=True)
        return east, west

    east_n, west_n = corner(tail_n)
    east_s, west_s = corner(tail_s)
    halves = []
    for k in range(2):
        at = slice(k * members, (k + 1) * members)
        a, b = cols_a[at, :], cols_b[at, :]
        from_e = jnp.where(f_even, a, b)
        from_w = jnp.where(f_even, b, a)
        close = jnp.where(even_lane, from_e, from_w)
        far = jnp.where(even_lane, pltpu.roll(from_e, cols - 1, 1), pltpu.roll(from_w, 1, 1))
        near[at, :] = close
        halves.append((close, far))
    wa, wb = cols_a[2 * members:, :], cols_b[2 * members:, :]
    w_e = jnp.where(f_even, wa, wb)
    w_w = jnp.where(f_even, wb, wa)
    w_packed = jnp.where(lanes((TAIL, cols)) % 2 == 0, w_e, w_w)
    near0, near1 = halves[0][0], halves[1][0]
    down0, down1 = pltpu.roll(near0, 2, 1), pltpu.roll(near1, 2, 1)
    up0, up1 = pltpu.roll(near0, cols - 2, 1), pltpu.roll(near1, cols - 2, 1)
    n0 = jnp.where(lane < 2, jnp.where(even_lane, east_n, west_n), down0)
    n1 = jnp.where(lane < 2, down0, down1)
    s0 = jnp.where(lane >= cols - 2, up1, up0)
    s1 = jnp.where(lane >= cols - 2, jnp.where(even_lane, east_s, west_s), up1)
    for k, (n, s) in enumerate(((n0, s0), (n1, s1))):
        at = slice(k * members, (k + 1) * members)
        close, far = halves[k]
        around = (n + s) + (far + own[at, :])
        halo1[at, :] = close + KAPPA * w_packed[k:k + 1, :] * (around - 4.0 * close)
    beside[0:members, :] = jnp.where(lane == 0, west_n, east_n)
    beside[members:2 * members, :] = pltpu.roll(near1, cols - 1, 1)
    beside[2 * members:3 * members, :] = pltpu.roll(near0, 1, 1)
    beside[3 * members:, :] = jnp.where(lane == 0, west_s, east_s)

    stride = CAP * members + TAGS
    tag_lane = lanes((TAGS, cols))
    for t in range(bands):
        counts[t] = 0
        sent[t * stride + CAP * members:(t + 1) * stride, :] = jnp.full((TAGS, cols), -1.0, BF16)
    half = rows // 2
    first, last = lane == 0, lane == cols - 1

    def field_row(r):
        inside = turned[jnp.clip(r, 0, rows - 1)]
        outside = strips[jnp.clip(jnp.where(r < 0, r + 2, r - rows + 2), 0, 3)]
        return jnp.where(jnp.logical_and(r >= 0, r < rows), inside, outside)

    def halo_row(ref, r):
        k = jnp.where(r >= half, 1, 0)
        at = pl.ds(pl.multiple_of(k * members, 8), members)
        return pltpu.roll(ref[at, :], cols - 1 - 2 * (r - k * half), 1)

    def side_row(r):
        edge = jnp.where(r < 0, beside[0:members, :], beside[3 * members:, :])
        inside = halo_row(near, jnp.clip(r, 0, rows - 1))
        return jnp.where(jnp.logical_and(r >= 0, r < rows), inside, edge)

    def relax(c, n, s, h, w):
        west = jnp.where(first, h, pltpu.roll(c, 1, 1))
        east = jnp.where(last, h, pltpu.roll(c, cols - 1, 1))
        return c + w * ((n + s) + (west + east) - 4.0 * c)

    def coef_row(r):
        at = jnp.where(r < 0, 0, r + 8)
        return coef[pl.ds(at, 1), :]

    def one(h):
        r = hub_row[h]
        u = [field_row(r + k) for k in range(-2, 3)]
        v = [relax(u[k + 2], u[k + 1], u[k + 3], side_row(r + k), coef_row(r + k)) for k in range(-1, 2)]
        moved = share[h] * relax(v[1], v[0], v[2], halo_row(halo1, r), coef_row(r))
        to = dest_tile[h]
        n = counts[to]
        counts[to] = n + 1
        base = pl.multiple_of(to * stride, 16)
        sent[pl.ds(pl.multiple_of(base + n * members, 16), members), :] = moved.astype(BF16)
        at = pl.ds(pl.multiple_of(base + CAP * members, 16), TAGS)
        tags = sent[at, :].astype(F32)
        tags = jnp.where(tag_lane == n, dest_row[h].astype(F32), tags)
        tags = jnp.where(tag_lane == CAP + n, county[h].astype(F32), tags)
        sent[at, :] = tags.astype(BF16)

    def several(i, carry):
        for k in range(UNROLL):
            one(i * UNROLL + k)
        return carry

    lax.fori_loop(0, hub_row.shape[0] // UNROLL, several, 0)


def grow_kernel(draw, threshold, grow, draw_v, grow_v, limit_v, in_sem, out_sem, sem):
    chunk = draw.shape[0] // GROW
    limit = pltpu.make_async_copy(threshold, limit_v, sem)
    limit.start()

    def fetch(i, carry):
        at = pl.ds(i * chunk, chunk)
        pltpu.make_async_copy(draw.at[at], draw_v.at[at], in_sem.at[i]).start()
        return carry

    lax.fori_loop(0, GROW, fetch, 0)
    limit.wait()

    def work(i, carry):
        at = pl.ds(i * chunk, chunk)
        pltpu.make_async_copy(draw.at[at], draw_v.at[at], in_sem.at[i]).wait()
        for k in range(chunk):
            x = 0.5 * SHARPNESS * (draw_v[i * chunk + k].astype(F32) - limit_v[...])
            grow_v[i * chunk + k] = 0.5 * jnp.tanh(x) + 0.5
        pltpu.make_async_copy(grow_v.at[at], grow.at[at], out_sem).start()
        return carry

    lax.fori_loop(0, GROW, work, 0)
    pltpu.make_async_copy(grow_v, grow, out_sem).wait()


def bulk_kernel(
    hub_row, share, density, grow, coef, strips, near, halo1, beside,
    kept, field, inner, gate, factor, in_sem, gate_sem, out_sem,
):
    members, rows, cols = density.shape
    half = rows // 2
    step = STEP
    blocks = rows // step

    def fetch(i, carry):
        for k in range(step):
            r = i * step + k
            pltpu.make_async_copy(density.at[:, r, :], field.at[r + 2], in_sem.at[i]).start()
        return carry

    def fetch_gate(i, carry):
        for k in range(step):
            r = i * step + k
            pltpu.make_async_copy(grow.at[:, r, :], gate.at[r], gate_sem.at[i]).start()
        return carry

    lax.fori_loop(0, blocks, fetch, 0)
    lax.fori_loop(0, blocks, fetch_gate, 0)
    for k in range(2):
        field[k] = strips[k]
        field[rows + 2 + k] = strips[2 + k]

    def clear(i, carry):
        for k in range(8):
            factor[i * 8 + k] = 1.0
        return carry

    lax.fori_loop(0, rows // 8, clear, 0)

    def leave(h, carry):
        r = hub_row[h]
        factor[r] = factor[r] - share[h]
        return carry

    lax.fori_loop(0, hub_row.shape[0], leave, 0)

    side = (members, cols)
    lane = lanes(side)
    first, last = lane == 0, lane == cols - 1

    edge = jnp.logical_or(first, last)
    band = (cols, cols)
    beside_mask = (jnp.abs(lanes(band) - sublanes(band)) == 1).astype(BF16)

    def lateral(c):
        flat = c.reshape(-1, cols)
        high = flat.astype(BF16)
        low = (flat - high.astype(F32)).astype(BF16)
        both = jnp.dot(high, beside_mask, preferred_element_type=F32)
        return (both + jnp.dot(low, beside_mask, preferred_element_type=F32)).reshape(c.shape)

    def relax(c, n, s, h, w, across):
        return c + w * ((n + s) + (across + jnp.where(edge, h, 0.0)) - 4.0 * c)

    def halo_row(ref, part, r):
        at = pl.ds(pl.multiple_of(part * members, 8), members)
        return pltpu.roll(ref[at, :], cols - 1 - 2 * (r - part * half), 1)

    def landed(i):
        ready = field.at[pl.ds(i * step + 2, step)]
        pltpu.make_async_copy(ready, ready, in_sem.at[i]).wait()

    landed(0)
    inner[0] = relax(field[1], field[0], field[2], beside[:members, :], coef[0:1, :], lateral(field[1]))

    def early(i, carry):
        @pl.when(i < blocks - 1)
        def _():
            landed(i + 1)

        part = i // (half // step)
        across = lateral(field[pl.ds(i * step + 2, step)])
        for k in range(step):
            r = i * step + k
            inner[r + 1] = relax(
                field[r + 2], field[r + 1], field[r + 3], halo_row(near, part, r), coef[pl.ds(r + 8, 1), :], across[k])
        return carry

    lax.fori_loop(0, blocks, early, 0)
    inner[rows + 1] = relax(
        field[rows + 2], field[rows + 1], field[rows + 3], beside[3 * members:, :], coef[rows + 8:rows + 9, :],
        lateral(field[rows + 2]))

    def late(i, carry):
        ready = gate.at[pl.ds(i * step, step)]
        pltpu.make_async_copy(ready, ready, gate_sem.at[i]).wait()
        part = i // (half // step)
        across = lateral(inner[pl.ds(i * step + 1, step)])
        for k in range(step):
            r = i * step + k
            d = relax(
                inner[r + 1], inner[r], inner[r + 2], halo_row(halo1, part, r), coef[pl.ds(r + 8, 1), :], across[k])
            gate[r] = d * factor[r] * gate[r]
        for k in range(step):
            r = i * step + k
            pltpu.make_async_copy(gate.at[r], kept.at[:, r, :], out_sem).start()
        return carry

    lax.fori_loop(0, blocks, late, 0)
    pltpu.make_async_copy(gate, gate, out_sem).wait()


def table_kernel(place, *refs):
    blocks, (table, sem) = refs[:-2], refs[-2:]
    flow = place[3]
    per = blocks[0].shape[0]
    copies = []
    for i, ref in enumerate(blocks):
        at = jnp.bitwise_xor(flow, i) * per
        copies.append(pltpu.make_async_copy(ref, table.at[pl.ds(at, per)], sem))
    for copy in copies:
        copy.start()
    for copy in copies:
        copy.wait()


def land_kernel(
    landed, table, kept, grow, out,
    base, gate, carried, tags_v, tags_s, owner, lead, tag_sem, row_sem, out_sem,
):
    bands, cols = tags_v.shape
    stride = landed.shape[0] // bands
    members, rows, _ = kept.shape
    depth = table.shape[1] - TAGS
    slots = bands * CAP
    for t in range(bands):
        tags = landed[t * stride + CAP * members:(t + 1) * stride, :].astype(F32)
        tags_v[t:t + 1, :] = tags[:1].astype(jnp.int32)
    copy = pltpu.make_async_copy(tags_v, tags_s, tag_sem)
    copy.start()

    def clear(r, carry):
        owner[r] = -1
        return carry

    lax.fori_loop(0, rows, clear, 0, unroll=8)
    copy.wait()

    def fetch(row, s):
        return (pltpu.make_async_copy(out.at[:, row, :], base.at[s], row_sem),
                pltpu.make_async_copy(grow.at[:, row, :], gate.at[s], row_sem))

    def store(row, s):
        return pltpu.make_async_copy(base.at[s], out.at[:, row, :], out_sem)

    def claim(s, carry):
        row = tags_s[s // CAP, s % CAP]
        at = jnp.maximum(row, 0)
        mine = owner[at]
        fresh = jnp.logical_and(row >= 0, mine < 0)
        lead[s] = jnp.where(row < 0, -1, jnp.where(mine < 0, s, mine))

        @pl.when(fresh)
        def _():
            owner[at] = s
            for c in fetch(at, s):
                c.start()

        return carry

    lax.fori_loop(0, slots, claim, 0)

    def product(t, carry):
        for n in range(CAP):
            c = jnp.maximum(tags_s[t, CAP + n], 0)
            at = pl.ds(pl.multiple_of(t * stride + n * members, 16), members)
            x = jnp.dot(landed[at, :], table[c, :depth, :], preferred_element_type=F32)
            scale = table[c, depth:, :].astype(F32)[:1]
            carried[t * CAP + n] = (x * scale).astype(BF16).astype(F32)
        return carry

    lax.fori_loop(0, bands, product, 0, unroll=8)

    def arrive(s, carry):
        @pl.when(lead[s] == s)
        def _():
            for c in fetch(tags_s[s // CAP, s % CAP], s):
                c.wait()
        return carry

    lax.fori_loop(0, slots, arrive, 0)

    def add(s, carry):
        @pl.when(lead[s] >= 0)
        def _():
            to = lead[s]
            base[to] = base[to] + carried[s] * gate[to]
        return carry

    lax.fori_loop(0, slots, add, 0)

    def send(s, carry):
        @pl.when(lead[s] == s)
        def _():
            store(tags_s[s // CAP, s % CAP], s).start()
        return carry

    def sent(s, carry):
        @pl.when(lead[s] == s)
        def _():
            store(tags_s[s // CAP, s % CAP], s).wait()
        return carry

    lax.fori_loop(0, slots, send, 0)
    lax.fori_loop(0, slots, sent, 0)


def smem():
    return pl.BlockSpec(memory_space=pltpu.SMEM)


def vmem():
    return pl.BlockSpec(memory_space=pltpu.VMEM)


def anywhere():
    return pl.BlockSpec(memory_space=pl.ANY)


def hbm():
    return pl.BlockSpec(memory_space=pltpu.HBM)


def params(mib):
    return pltpu.CompilerParams(vmem_limit_bytes=int(mib * MIB))


def near_pairs(count):
    return [(i, i ^ 1) for i in range(count)]


def far_pairs(count):
    return [(i, j) for k in range(1, count - 1, 2) for i, j in ((k, k + 1), (k + 1, k))]


def local(
    density,
    habitat_class,
    suitability,
    dispersal_draw,
    threshold,
    hub_row,
    dest_tile,
    dest_row,
    county_id,
    jump_share,
    flow_tiles,
    flow_scale,
):
    members, rows, cols = density.shape
    bands, flows = lax.axis_size("tile"), lax.axis_size("flow")
    density, dispersal_draw, habitat_class, flow_tiles = (
        pltpu.with_memory_space_constraint(x, pltpu.HBM)
        for x in (density, dispersal_draw, habitat_class, flow_tiles))
    t, f = lax.axis_index("tile"), lax.axis_index("flow")
    place = jnp.stack([t % 2, f % 2, t, f]).astype(jnp.int32)
    hubs, share = hub_row.reshape(-1), jump_share.reshape(-1)
    sds = jax.ShapeDtypeStruct
    per, depth = flow_tiles.shape[:2]
    message = sds((2 * members + TAIL, cols), F32)
    pack = sds((2 * members, cols), F32)
    cols_a, cols_b, rows_a, rows_b, own, weight, tiles, turned = pl.pallas_call(
        edges_kernel,
        out_shape=(message, message, message, message, pack, sds((rows, cols), F32),
                   sds((per, depth + TAGS, cols), BF16), sds((rows, members, cols), F32)),
        in_specs=[smem()] + [hbm()] * 5,
        out_specs=(vmem(),) * 8,
        scratch_shapes=[
            pltpu.VMEM(pack.shape, F32),
            pltpu.VMEM(pack.shape, F32),
            pltpu.VMEM((rows, cols), jnp.int32),
            pltpu.SMEM(suitability.shape, F32),
            pltpu.VMEM((1, per), BF16),
            pltpu.SemaphoreType.DMA((rows // CHUNK,)),
            pltpu.SemaphoreType.DMA((4,)),
        ],
        compiler_params=params(24),
        name="edges",
    )(place, density, habitat_class, suitability, flow_tiles, flow_scale.reshape(1, -1))

    got_a = lax.ppermute(cols_a, "flow", near_pairs(flows))
    got_b = lax.ppermute(cols_b, "flow", far_pairs(flows))
    rows_a, rows_b = pl.pallas_call(
        corners_kernel,
        out_shape=(message, message),
        in_specs=[smem()] + [vmem()] * 4,
        out_specs=(vmem(), vmem()),
        compiler_params=params(24),
        name="corners",
    )(place, rows_a, rows_b, got_a, got_b)
    strip_a = lax.ppermute(rows_a, "tile", near_pairs(bands))
    strip_b = lax.ppermute(rows_b, "tile", far_pairs(bands))

    stride = CAP * members + TAGS
    sent, near, halo1, beside, coef, strips = pl.pallas_call(
        hubs_kernel,
        out_shape=(sds((bands * stride, cols), BF16), pack, pack, sds((4 * members, cols), F32),
                   sds((rows + 16, cols), F32), sds((4, members, cols), F32)),
        in_specs=[smem()] * 6 + [vmem()] * 7,
        out_specs=(vmem(),) * 6,
        scratch_shapes=[pltpu.SMEM((bands,), jnp.int32)],
        compiler_params=params(24),
        name="hubs",
    )(place, hubs, dest_tile.reshape(-1), dest_row.reshape(-1), county_id.reshape(-1), share,
      turned, weight, own, got_a, got_b, strip_a, strip_b)

    landed = lax.all_to_all(sent, "tile", split_axis=0, concat_axis=0, tiled=True)
    dispersal_draw, near = lax.optimization_barrier((dispersal_draw, near))
    blocks = [tiles]
    bit = flows // 2
    offsets = [0]
    while bit:
        blocks += [lax.ppermute(x, "flow", [(i, i ^ bit) for i in range(flows)]) for x in blocks]
        offsets += [o ^ bit for o in offsets]
        bit //= 2
    blocks = [x for _, x in sorted(zip(offsets, blocks), key=lambda p: p[0])]
    table = pl.pallas_call(
        table_kernel,
        out_shape=sds((flows * per, depth + TAGS, cols), BF16),
        in_specs=[smem()] + [vmem()] * flows,
        out_specs=vmem(),
        scratch_shapes=[pltpu.SemaphoreType.DMA],
        compiler_params=params(24),
        name="table",
    )(place, *blocks)

    grow = pl.pallas_call(
        grow_kernel,
        out_shape=sds(density.shape, F32),
        in_specs=[hbm(), hbm()],
        out_specs=hbm(),
        scratch_shapes=[
            pltpu.VMEM(density.shape, BF16),
            pltpu.VMEM(density.shape, F32),
            pltpu.VMEM((rows, cols), F32),
            pltpu.SemaphoreType.DMA((GROW,)),
            pltpu.SemaphoreType.DMA,
            pltpu.SemaphoreType.DMA,
        ],
        compiler_params=params(24),
        name="grow",
    )(dispersal_draw, threshold)
    grow = pltpu.with_memory_space_constraint(grow, pltpu.HBM)

    kept = pl.pallas_call(
        bulk_kernel,
        out_shape=sds(density.shape, F32),
        in_specs=[smem(), smem(), hbm(), hbm()] + [vmem()] * 5,
        out_specs=hbm(),
        scratch_shapes=[
            pltpu.VMEM((rows + 4, members, cols), F32),
            pltpu.VMEM((rows + 2, members, cols), F32),
            pltpu.VMEM((rows, members, cols), F32),
            pltpu.SMEM((rows,), F32),
            pltpu.SemaphoreType.DMA((rows // STEP,)),
            pltpu.SemaphoreType.DMA((rows // STEP,)),
            pltpu.SemaphoreType.DMA,
        ],
        compiler_params=params(24),
        name="bulk",
    )(hubs, share, density, grow, coef, strips, near, halo1, beside)

    slots = bands * CAP
    out = pl.pallas_call(
        land_kernel,
        out_shape=sds(density.shape, F32),
        in_specs=[vmem(), vmem(), hbm(), hbm()],
        out_specs=hbm(),
        input_output_aliases={2: 0},
        scratch_shapes=[
            pltpu.VMEM((slots, members, cols), F32),
            pltpu.VMEM((slots, members, cols), F32),
            pltpu.VMEM((slots, members, cols), F32),
            pltpu.VMEM((bands, cols), jnp.int32),
            pltpu.SMEM((bands, cols), jnp.int32),
            pltpu.SMEM((rows,), jnp.int32),
            pltpu.SMEM((slots,), jnp.int32),
            pltpu.SemaphoreType.DMA,
            pltpu.SemaphoreType.DMA,
            pltpu.SemaphoreType.DMA,
        ],
        compiler_params=params(24),
        name="land",
    )(landed, table, kept, grow)
    return out


def solution(mesh):
    in_specs = (
        P(None, "tile", "flow"),
        P("tile", "flow"),
        P(),
        P(None, "tile", "flow"),
        P("tile", "flow"),
        P("flow", "tile"),
        P("flow", "tile", None),
        P("flow", "tile"),
        P("flow", "tile"),
        P("flow", "tile"),
        P("flow", None, None),
        P("flow"),
    )
    out_specs = P(None, "tile", "flow")
    return jax.shard_map(local, mesh=mesh, in_specs=in_specs, out_specs=out_specs, check_vma=False)
```

time: 195 us -> 54.5 us (0.28)
  other arithmetic: 65.2 us -> 0.08 us
  local copies, waits for them, and re-layouts: 57.5 us -> 3.28 us
  Pallas kernels: 0 us -> 24.8 us
  blocking collectives: 15.2 us -> 0 us
  starting transfers between devices: 34.5 us -> 20.7 us
  matrix products: 13 us -> 0 us
  waiting for transfers between devices: 7.44 us -> 4.84 us
    add x3 -> x0, other arithmetic: 43.1 us -> none  [the longest x2 43.1 us: relax(): return centre + KAPPA * centre_weight * (beside_all - 4.0 * centre)]
    pallas_call x0 -> x7, Pallas kernels: none -> 24.8 us  [the longest x1 8.7 us: local(): pl.pallas_call(bulk_kernel, out_shape=sds(density.shape, F32), in_specs=[...]
    slice x6 -> x0, local copies, waits for them, and re-layouts: 18.4 us -> none  [the longest x3 10.6 us: with_halo(): lax.slice_in_dim(cells, cells.shape[dim] - width, cells.shape[dim], axis=...]
    dot_general x4 -> x0, matrix products: 13 us -> none  [the longest x1 7.25 us: local(): jnp.einsum('sr,smk->mrk', landing, landed, preferred_element_type=jnp.flo...]
    mul x2 -> x0, other arithmetic: 11.4 us -> none  [the longest x1 10.2 us: relax(): return centre + KAPPA * centre_weight * (beside_all - 4.0 * centre)]
    ppermute x8 -> x7, starting transfers between devices: 23.2 us -> 11.9 us  [the longest x3 4.73 us: local(): lax.ppermute(x, 'flow', [(i, i ^ bit) for i in range(flows)])]
    ppermute x4 -> x0, local copies, waits for them, and re-layouts: 10.9 us -> none  [the longest x2 5.45 us: with_halo(): lax.ppermute(tail, axis, [(i, (i + 1) % count) for i in range(ends)])]
    all_gather x1 -> x0, blocking collectives: 8.62 us -> none  [local(): lax.all_gather(flow_tiles, 'flow', axis=0, tiled=True)]
  transfers between devices with their start and end apart: 10 -> 8, of which waited for: 3 -> 3; matrix products, arithmetic and copies ran while one was open for 48% -> 0% of each run, Pallas kernels for 0% -> 23%
where the time goes in v1:
time: 54.5 us; the launch traced here: 53.9 us
  Pallas kernels  24.8 us (46%)
  starting transfers between devices  20.7 us (38%)
  waiting for transfers between devices  4.84 us (9%)
  local copies, waits for them, and re-layouts  3.28 us (6%)
    all_to_all x1, starting transfers between devices, local(): lax.all_to_all(sent, 'tile', split_axis=0, concat_axis=0, tiled=True)  8.83 us
    pallas_call x1, Pallas kernels, local(): pl.pallas_call(bulk_kernel, out_shape=sds(density.shape, F32), in_specs=[...  8.7 us
    ppermute x3, starting transfers between devices, local(): lax.ppermute(x, 'flow', [(i, i ^ bit) for i in range(flows)])  4.73 us
    ppermute x1, starting transfers between devices, local(): got_b = lax.ppermute(cols_b, 'flow', far_pairs(flows))  4.48 us
    pallas_call x1, Pallas kernels, local(): pl.pallas_call(hubs_kernel, out_shape=(sds((bands * stride, cols), BF16),...  4.11 us
    pallas_call x1, Pallas kernels, local(): pl.pallas_call(land_kernel, out_shape=sds(density.shape, F32), in_specs=[...  3.76 us
    pallas_call x1, Pallas kernels, local(): pl.pallas_call(edges_kernel, out_shape=(message, message, message, messag...  3.75 us
    unnamed x18, local copies, waits for them, and re-layouts  3.28 us
  transfers between devices with their start and end apart: 8, of which 3 were waited for; matrix products, arithmetic and copies ran while one was open for 0% of the time, Pallas kernels for 23%

profile of v1, /device:TPU:1, one launch (start us, length us, event | category | flops | bytes accessed | tf_op | source)
XLA Modules:
  0.0 53.9 jit_solution(1949254334421049041)
XLA Ops:
  0.0 0.1 pad_add_fusion.place
  0.1 0.7 %copy-done.4 = f32[16]{0:T(128)S(1)} copy-done((f32[16]{0:T(128)S(1)}, f32[16]{0:T(128)}, u32[]{:S(2)}) %copy-start.4) | copy-done | bytes 88
  0.8 0.7 %copy-done.5 = bf16[4]{0:T(256)(128)(2,1)S(1)} copy-done((bf16[4]{0:T(256)(128)(2,1)S(1)}, bf16[4]{0:T(256)(128)(2,1)}, u32[]{:S(2)}) %copy-start.5) | copy-done | bytes 32
  1.4 3.7 %edges.1 = (f32[136,128]{1,0:T(8,128)S(1)}, f32[136,128]{1,0:T(8,128)S(1)}, f32[136,128]{1,0:T(8,128)S(1)}, f32[136,128]{1,0:T(8,128)S(1)}, f32[128,128]{1,0:T(8...) custom-call(s32[4]{0:T(128)S(1)} %pad_add_fusion.place, ...), custom_call_target="tpu_custom_call" | custom-call | tf_op jit(solution)/shard_map/edges/pallas_call | solution.py:559
  5.2 0.1 collective-permute-start
  5.3 4.5 %collective-permute-start.1 = (f32[136,128]{1,0:T(8,128)S(1)}, f32[136,128]{1,0:T(8,128)S(1)}, u32[]{:S(2)}, u32[]{:S(2)}) collective-permute-start(f32[136,128]{1,0:T(8,128)S(1)} %get-tuple-element.27), channel_id=1, source_target_pairs={{1,2},{2,1},{5,6},{6,5},{9,10},{10,9},{13,14},{14,13},{17,18},{18,... | collective-permute-start | bytes 208904 | tf_op jit(solution)/shard_map/ppermute | solution.py:579
  9.8 0.0 collective-permute-done.got_a.cols_a
  9.8 2.3 %collective-permute-done.1.got_b.cols_b = f32[136,128]{1,0:T(8,128)S(1)} collective-permute-done((f32[136,128]{1,0:T(8,128)S(1)}, f32[136,128]{1,0:T(8,128)S(1)}, u32[]{:S(2)}, u32[]{:S(2)}) %collective-permute-start.1) | collective-permute-done | bytes 69664 | tf_op jit(solution)/shard_map/ppermute | solution.py:579
  12.1 0.7 %corners.1 = (f32[136,128]{1,0:T(8,128)S(1)}, f32[136,128]{1,0:T(8,128)S(1)}) custom-call(s32[4]{0:T(128)S(1)} %pad_add_fusion.place, f32[136,128]{1,0:T(8,128)S(1)} %get-tuple-element.28.rows_a, f32[136,128]{1,0:T(8,128)S(1)} %get-tuple-element.29.rows_b, f32[136,128]{1,0:T(8,128)S(1)} %collective-permute-done.got_a.cols_a, ...), custom_call_target="tpu_custom_call" | custom-call | tf_op jit(solution)/shard_map/corners/pallas_call | solution.py:580
  12.7 1.9 %collective-permute-start.2 = (f32[136,128]{1,0:T(8,128)S(1)}, f32[136,128]{1,0:T(8,128)S(1)}, u32[]{:S(2)}, u32[]{:S(2)}) collective-permute-start(f32[136,128]{1,0:T(8,128)S(1)} %get-tuple-element.30), channel_id=1, source_target_pairs={{0,4},{4,0},{8,12},{12,8},{16,20},{20,16},{24,28},{28,24},{1,5},{5... | collective-permute-start | bytes 208904 | tf_op jit(solution)/shard_map/ppermute | solution.py:588
  14.7 0.7 %collective-permute-start.3 = (f32[136,128]{1,0:T(8,128)S(1)}, f32[136,128]{1,0:T(8,128)S(1)}, u32[]{:S(2)}, u32[]{:S(2)}) collective-permute-start(f32[136,128]{1,0:T(8,128)S(1)} %get-tuple-element.31), channel_id=1, source_target_pairs={{4,8},{8,4},{12,16},{16,12},{20,24},{24,20},{5,9},{9,5},{13,17},{1... | collective-permute-start | bytes 208904 | tf_op jit(solution)/shard_map/ppermute | solution.py:589
  15.3 1.0 %collective-permute-done.2.rows_a = f32[136,128]{1,0:T(8,128)S(1)} collective-permute-done((f32[136,128]{1,0:T(8,128)S(1)}, f32[136,128]{1,0:T(8,128)S(1)}, u32[]{:S(2)}, u32[]{:S(2)}) %collective-permute-start.2) | collective-permute-done | bytes 69664 | tf_op jit(solution)/shard_map/ppermute | solution.py:588
  16.4 0.0 collective-permute-done.3.rows_b
  16.4 4.1 %hubs.1 = (bf16[2176,128]{1,0:T(8,128)(2,1)}, f32[128,128]{1,0:T(8,128)S(1)}, f32[128,128]{1,0:T(8,128)S(1)}, f32[256,128]{1,0:T(8,128)S(1)}, f32[144,128]{1,0:T(8,128)S(1)}, /*index=5*/f32[4,64,128]{2,1,0:T(8,128)S(1)}) custom-call(s32[4]{0:T(128)S(1)} %pad_add_fusion.place, s32[16]{0:T(128)S(1)} %bitcast.13, s32[16]{0:T(128)S(1)} %bitcast.18, ...), custom_call_target="tpu_custom_call" | custom-call | tf_op jit(solution)/shard_map/hubs/pallas_call | solution.py:592
  20.5 8.8 %all-to-all-start = ((bf16[8,272,128]{2,1,0:T(8,128)(2,1)}), bf16[8,272,128]{2,1,0:T(8,128)(2,1)S(1)}, u32[]{:S(2)}, u32[]{:S(2)}) async-start(bf16[8,272,128]{2,1,0:T(8,128)(2,1)} %bitcast.10), calls=%async_computation | async-start | bytes 1114112 | tf_op jit(solution)/shard_map/all_to_all | solution.py:604
  29.3 2.9 %collective-permute-start.4 = (bf16[4,144,128]{2,1,0:T(8,128)(2,1)S(1)}, bf16[4,144,128]{2,1,0:T(8,128)(2,1)S(1)}, u32[]{:S(2)}, u32[]{:S(2)}) collective-permute-start(bf16[4,144,128]{2,1,0:T(8,128)(2,1)S(1)} %get-tuple-element.33.refs_0_), channel_id=1, source_target_pairs={{0,1},{1,0},{2,3},{3,2},{4,5},{5,4},{6,7},{7,6},{8,9},{9,8},{10,11... | collective-permute-start | bytes 442376 | tf_op jit(solution)/shard_map/ppermute | solution.py:610
  32.3 1.5 %collective-permute-done.5.refs_2_ = bf16[4,144,128]{2,1,0:T(8,128)(2,1)S(1)} collective-permute-done((bf16[4,144,128]{2,1,0:T(8,128)(2,1)S(1)}, bf16[4,144,128]{2,1,0:T(8,128)(2,1)S(1)}, u32[]{:S(2)}, u32[]{:S(2)}) %collective-permute-start.5) | collective-permute-done | bytes 147488 | tf_op jit(solution)/shard_map/ppermute | solution.py:610
  33.8 1.8 %collective-permute-start.6 = (bf16[4,144,128]{2,1,0:T(8,128)(2,1)S(1)}, bf16[4,144,128]{2,1,0:T(8,128)(2,1)S(1)}, u32[]{:S(2)}, u32[]{:S(2)}) collective-permute-start(bf16[4,144,128]{2,1,0:T(8,128)(2,1)S(1)} %collective-permute-done.5.refs_2_), channel_id=1, source_target_pairs={{0,1},{1,0},{2,3},{3,2},{4,5},{5,4},{6,7},{7,6},{8,9},{9,8},{10,11... | collective-permute-start | bytes 442376 | tf_op jit(solution)/shard_map/ppermute | solution.py:610
  35.6 2.5 %grow.1 = f32[64,128,128]{2,1,0:T(8,128)S(1)} custom-call(bf16[64,128,128]{2,1,0:T(8,128)(2,1)} %draw, f32[128,128]{1,0:T(8,128)S(1)} %copy-done.1), custom_call_target="tpu_custom_call" | custom-call | tf_op jit(solution)/shard_map/grow/pallas_call | solution.py:624
  38.1 1.9 %copy-done = f32[64,128,128]{2,1,0:T(8,128)} copy-done((f32[64,128,128]{2,1,0:T(8,128)}, f32[64,128,128]{2,1,0:T(8,128)S(1)}, u32[]{:S(2)}) %copy-start) | copy-done | bytes 4194328
  40.0 8.7 %bulk.1.kept = f32[64,128,128]{2,1,0:T(8,128)} custom-call(s32[16]{0:T(128)S(1)} %bitcast.14, f32[16]{0:T(128)S(1)} %bitcast.16, f32[64,128,128]{2,1,0:T(8,128)} %density.3, f32[64,128,128]{2,1,0:T(8,128)} %copy-done, f32[144,128]{1,0:T(8,128)S(1)} %get-tuple-element.36.coef, f32[4,64,128]{2,1,0:T(8,128)S(1)} %get-tuple-element.37.strips, ...), custom_call_target="tpu_custom_call" | custom-call | tf_op jit(solution)/shard_map/bulk/pallas_call | solution.py:642
  48.8 1.3 %table.1 = bf16[16,144,128]{2,1,0:T(8,128)(2,1)S(1)} custom-call(s32[4]{0:T(128)S(1)} %pad_add_fusion.place, bf16[4,144,128]{2,1,0:T(8,128)(2,1)S(1)} %get-tuple-element.33.refs_0_, bf16[4,144,128]{2,1,0:T(8,128)(2,1)S(1)} %collective-permute-done.4.refs_1_, bf16[4,144,128]{2,1,0:T(8,128)(2,1)S(1)} %collective-permute-done.5.refs_2_, ...), custom_call_target="tpu_custom_call" | custom-call | tf_op jit(solution)/shard_map/table/pallas_call | solution.py:614
  50.1 0.0 all-to-all-done
  50.1 3.8 %land.1 = f32[64,128,128]{2,1,0:T(8,128)} custom-call(bf16[2176,128]{1,0:T(8,128)(2,1)S(1)} %bitcast.12, bf16[16,144,128]{2,1,0:T(8,128)(2,1)S(1)} %table.1, f32[64,128,128]{2,1,0:T(8,128)} %bulk.1.kept, f32[64,128,128]{2,1,0:T(8,128)} %copy-done), custom_call_target="tpu_custom_call", output_to_operand_aliasing={{}: (2, {})} | custom-call | tf_op jit(solution)/shard_map/land/pallas_call | solution.py:661
  (18 shorter events, 0.0 us)
Async XLA Ops:
  0.0 16.4 %copy-start.3 = (f32[1,16]{1,0:T(1,128)S(1)}, f32[1,16]{1,0:T(1,128)}, u32[]{:S(2)}) copy-start(f32[1,16]{1,0:T(1,128)} %param.21) | copy-start | bytes 196
  0.0 16.4 %copy-start.8 = (s32[1,16]{1,0:T(1,128)S(1)}, s32[1,16]{1,0:T(1,128)}, u32[]{:S(2)}) copy-start(s32[1,16]{1,0:T(1,128)} %param.20) | copy-start | bytes 196
  0.0 16.4 %copy-start.7 = (s32[1,16]{1,0:T(1,128)S(1)}, s32[1,16]{1,0:T(1,128)}, u32[]{:S(2)}) copy-start(s32[1,16]{1,0:T(1,128)} %param.19) | copy-start | bytes 196
  0.0 16.4 %copy-start.6 = (s32[1,16,1]{1,2,0:T(1,128)S(1)}, s32[1,16,1]{1,2,0:T(1,128)}, u32[]{:S(2)}) copy-start(s32[1,16,1]{1,2,0:T(1,128)} %param.18) | copy-start | bytes 196
  0.0 16.4 %copy-start.2 = (s32[1,16]{1,0:T(1,128)S(1)}, s32[1,16]{1,0:T(1,128)}, u32[]{:S(2)}) copy-start(s32[1,16]{1,0:T(1,128)} %param.17) | copy-start | bytes 196
  0.1 0.7 %copy-start.4 = (f32[16]{0:T(128)S(1)}, f32[16]{0:T(128)}, u32[]{:S(2)}) copy-start(f32[16]{0:T(128)} %suit.1) | copy-start | bytes 196
  0.8 0.7 %copy-start.5 = (bf16[4]{0:T(256)(128)(2,1)S(1)}, bf16[4]{0:T(256)(128)(2,1)}, u32[]{:S(2)}) copy-start(bf16[4]{0:T(256)(128)(2,1)} %param.23) | copy-start | bytes 28
  1.4 34.2 %copy-start.1 = (f32[128,128]{1,0:T(8,128)S(1)}, f32[128,128]{1,0:T(8,128)}, u32[]{:S(2)}) copy-start(f32[128,128]{1,0:T(8,128)} %threshold.1) | copy-start | bytes 196612
  5.2 4.6 %collective-permute-start = (f32[136,128]{1,0:T(8,128)S(1)}, f32[136,128]{1,0:T(8,128)S(1)}, u32[]{:S(2)}, u32[]{:S(2)}) collective-permute-start(f32[136,128]{1,0:T(8,128)S(1)} %get-tuple-element.26), channel_id=1, source_target_pairs={{0,1},{1,0},{2,3},{3,2},{4,5},{5,4},{6,7},{7,6},{8,9},{9,8},{10,11... | collective-permute-start | bytes 208904 | tf_op jit(solution)/shard_map/ppermute | solution.py:578
  5.3 6.8 %collective-permute-start.1 = (f32[136,128]{1,0:T(8,128)S(1)}, f32[136,128]{1,0:T(8,128)S(1)}, u32[]{:S(2)}, u32[]{:S(2)}) collective-permute-start(f32[136,128]{1,0:T(8,128)S(1)} %get-tuple-element.27), channel_id=1, source_target_pairs={{1,2},{2,1},{5,6},{6,5},{9,10},{10,9},{13,14},{14,13},{17,18},{18,... | collective-permute-start | bytes 208904 | tf_op jit(solution)/shard_map/ppermute | solution.py:579
  12.7 3.6 %collective-permute-start.2 = (f32[136,128]{1,0:T(8,128)S(1)}, f32[136,128]{1,0:T(8,128)S(1)}, u32[]{:S(2)}, u32[]{:S(2)}) collective-permute-start(f32[136,128]{1,0:T(8,128)S(1)} %get-tuple-element.30), channel_id=1, source_target_pairs={{0,4},{4,0},{8,12},{12,8},{16,20},{20,16},{24,28},{28,24},{1,5},{5... | collective-permute-start | bytes 208904 | tf_op jit(solution)/shard_map/ppermute | solution.py:588
  14.7 1.7 %collective-permute-start.3 = (f32[136,128]{1,0:T(8,128)S(1)}, f32[136,128]{1,0:T(8,128)S(1)}, u32[]{:S(2)}, u32[]{:S(2)}) collective-permute-start(f32[136,128]{1,0:T(8,128)S(1)} %get-tuple-element.31), channel_id=1, source_target_pairs={{4,8},{8,4},{12,16},{16,12},{20,24},{24,20},{5,9},{9,5},{13,17},{1... | collective-permute-start | bytes 208904 | tf_op jit(solution)/shard_map/ppermute | solution.py:589
  20.5 29.6 %all-to-all-start = ((bf16[8,272,128]{2,1,0:T(8,128)(2,1)}), bf16[8,272,128]{2,1,0:T(8,128)(2,1)S(1)}, u32[]{:S(2)}, u32[]{:S(2)}) async-start(bf16[8,272,128]{2,1,0:T(8,128)(2,1)} %bitcast.10), calls=%async_computation | async-start | bytes 1114112 | tf_op jit(solution)/shard_map/all_to_all | solution.py:604
  29.3 4.5 %collective-permute-start.5 = (bf16[4,144,128]{2,1,0:T(8,128)(2,1)S(1)}, bf16[4,144,128]{2,1,0:T(8,128)(2,1)S(1)}, u32[]{:S(2)}, u32[]{:S(2)}) collective-permute-start(bf16[4,144,128]{2,1,0:T(8,128)(2,1)S(1)} %get-tuple-element.33.refs_0_), channel_id=1, source_target_pairs={{0,2},{1,3},{2,0},{3,1},{4,6},{5,7},{6,4},{7,5},{8,10},{9,11},{10,... | collective-permute-start | bytes 442376 | tf_op jit(solution)/shard_map/ppermute | solution.py:610
  29.3 19.4 %collective-permute-start.4 = (bf16[4,144,128]{2,1,0:T(8,128)(2,1)S(1)}, bf16[4,144,128]{2,1,0:T(8,128)(2,1)S(1)}, u32[]{:S(2)}, u32[]{:S(2)}) collective-permute-start(bf16[4,144,128]{2,1,0:T(8,128)(2,1)S(1)} %get-tuple-element.33.refs_0_), channel_id=1, source_target_pairs={{0,1},{1,0},{2,3},{3,2},{4,5},{5,4},{6,7},{7,6},{8,9},{9,8},{10,11... | collective-permute-start | bytes 442376 | tf_op jit(solution)/shard_map/ppermute | solution.py:610
  33.8 15.0 %collective-permute-start.6 = (bf16[4,144,128]{2,1,0:T(8,128)(2,1)S(1)}, bf16[4,144,128]{2,1,0:T(8,128)(2,1)S(1)}, u32[]{:S(2)}, u32[]{:S(2)}) collective-permute-start(bf16[4,144,128]{2,1,0:T(8,128)(2,1)S(1)} %collective-permute-done.5.refs_2_), channel_id=1, source_target_pairs={{0,1},{1,0},{2,3},{3,2},{4,5},{5,4},{6,7},{7,6},{8,9},{9,8},{10,11... | collective-permute-start | bytes 442376 | tf_op jit(solution)/shard_map/ppermute | solution.py:610
  38.1 1.9 %copy-start = (f32[64,128,128]{2,1,0:T(8,128)}, f32[64,128,128]{2,1,0:T(8,128)S(1)}, u32[]{:S(2)}) copy-start(f32[64,128,128]{2,1,0:T(8,128)S(1)} %grow.1) | copy-start | bytes 12582916

commit v2 on v1

--- a/solution.py
+++ b/solution.py
@@ -231,34 +231,47 @@
         inside = halo_row(near, jnp.clip(r, 0, rows - 1))
         return jnp.where(jnp.logical_and(r >= 0, r < rows), inside, edge)
 
-    def relax(c, n, s, h, w):
-        west = jnp.where(first, h, pltpu.roll(c, 1, 1))
-        east = jnp.where(last, h, pltpu.roll(c, cols - 1, 1))
-        return c + w * ((n + s) + (west + east) - 4.0 * c)
+    edge = jnp.logical_or(first, last)
+    band = (cols, cols)
+    mask = (jnp.abs(lanes(band) - sublanes(band)) == 1).astype(BF16)
+
+    def lateral(rows_in):
+        flat = jnp.concatenate(rows_in, axis=0)
+        high = flat.astype(BF16)
+        low = (flat - high.astype(F32)).astype(BF16)
+        both = jnp.dot(high, mask, preferred_element_type=F32) + jnp.dot(low, mask, preferred_element_type=F32)
+        return [both[k * members:(k + 1) * members] for k in range(len(rows_in))]
+
+    def relax(c, n, s, h, w, across):
+        return c + w * ((n + s) + (across + jnp.where(edge, h, 0.0)) - 4.0 * c)
 
     def coef_row(r):
         at = jnp.where(r < 0, 0, r + 8)
         return coef[pl.ds(at, 1), :]
 
-    def one(h):
-        r = hub_row[h]
-        u = [field_row(r + k) for k in range(-2, 3)]
-        v = [relax(u[k + 2], u[k + 1], u[k + 3], side_row(r + k), coef_row(r + k)) for k in range(-1, 2)]
-        moved = share[h] * relax(v[1], v[0], v[2], halo_row(halo1, r), coef_row(r))
-        to = dest_tile[h]
-        n = counts[to]
-        counts[to] = n + 1
-        base = pl.multiple_of(to * stride, 16)
-        sent[pl.ds(pl.multiple_of(base + n * members, 16), members), :] = moved.astype(BF16)
-        at = pl.ds(pl.multiple_of(base + CAP * members, 16), TAGS)
-        tags = sent[at, :].astype(F32)
-        tags = jnp.where(tag_lane == n, dest_row[h].astype(F32), tags)
-        tags = jnp.where(tag_lane == CAP + n, county[h].astype(F32), tags)
-        sent[at, :] = tags.astype(BF16)
-
     def several(i, carry):
-        for k in range(UNROLL):
-            one(i * UNROLL + k)
+        chosen = [i * UNROLL + k for k in range(UNROLL)]
+        spot = [hub_row[h] for h in chosen]
+        u = [[field_row(r + k) for k in range(-2, 3)] for r in spot]
+        across = lateral([u[k][c] for k in range(UNROLL) for c in (1, 2, 3)])
+        v = []
+        for k, r in enumerate(spot):
+            v.append([
+                relax(u[k][c + 2], u[k][c + 1], u[k][c + 3], side_row(r + c), coef_row(r + c), across[3 * k + c + 1])
+                for c in range(-1, 2)])
+        across = lateral([x[1] for x in v])
+        for k, (h, r) in enumerate(zip(chosen, spot)):
+            moved = share[h] * relax(v[k][1], v[k][0], v[k][2], halo_row(halo1, r), coef_row(r), across[k])
+            to = dest_tile[h]
+            n = counts[to]
+            counts[to] = n + 1
+            base = pl.multiple_of(to * stride, 16)
+            sent[pl.ds(pl.multiple_of(base + n * members, 16), members), :] = moved.astype(BF16)
+            at = pl.ds(pl.multiple_of(base + CAP * members, 16), TAGS)
+            tags = sent[at, :].astype(F32)
+            tags = jnp.where(tag_lane == n, dest_row[h].astype(F32), tags)
+            tags = jnp.where(tag_lane == CAP + n, county[h].astype(F32), tags)
+            sent[at, :] = tags.astype(BF16)
         return carry
 
     lax.fori_loop(0, hub_row.shape[0] // UNROLL, several, 0)
@@ -397,24 +410,10 @@
     pltpu.make_async_copy(gate, gate, out_sem).wait()
 
 
-def table_kernel(place, *refs):
-    blocks, (table, sem) = refs[:-2], refs[-2:]
-    flow = place[3]
+def land_kernel(place, landed, kept, grow, *rest):
+    blocks, rest = rest[:-12], rest[-12:]
+    out, table, base, gate, carried, tags_v, tags_s, owner, lead, tag_sem, row_sem, out_sem = rest
     per = blocks[0].shape[0]
-    copies = []
-    for i, ref in enumerate(blocks):
-        at = jnp.bitwise_xor(flow, i) * per
-        copies.append(pltpu.make_async_copy(ref, table.at[pl.ds(at, per)], sem))
-    for copy in copies:
-        copy.start()
-    for copy in copies:
-        copy.wait()
-
-
-def land_kernel(
-    landed, table, kept, grow, out,
-    base, gate, carried, tags_v, tags_s, owner, lead, tag_sem, row_sem, out_sem,
-):
     bands, cols = tags_v.shape
     stride = landed.shape[0] // bands
     members, rows, _ = kept.shape
@@ -425,12 +424,17 @@
         tags_v[t:t + 1, :] = tags[:1].astype(jnp.int32)
     copy = pltpu.make_async_copy(tags_v, tags_s, tag_sem)
     copy.start()
+    for d, ref in enumerate(blocks):
+        at = jnp.bitwise_xor(place[3], d) * per
+        for c in range(per):
+            table[at + c] = ref[c]
 
     def clear(r, carry):
-        owner[r] = -1
-        return carry
-
-    lax.fori_loop(0, rows, clear, 0, unroll=8)
+        for k in range(8):
+            owner[r * 8 + k] = -1
+        return carry
+
+    lax.fori_loop(0, rows // 8, clear, 0)
     copy.wait()
 
     def fetch(row, s):
@@ -440,12 +444,12 @@
     def store(row, s):
         return pltpu.make_async_copy(base.at[s], out.at[:, row, :], out_sem)
 
-    def claim(s, carry):
+    def claim(s, count):
         row = tags_s[s // CAP, s % CAP]
         at = jnp.maximum(row, 0)
         mine = owner[at]
         fresh = jnp.logical_and(row >= 0, mine < 0)
-        lead[s] = jnp.where(row < 0, -1, jnp.where(mine < 0, s, mine))
+        lead[s] = jnp.where(row < 0, slots, jnp.where(mine < 0, s, mine))
 
         @pl.when(fresh)
         def _():
@@ -453,9 +457,9 @@
             for c in fetch(at, s):
                 c.start()
 
-        return carry
-
-    lax.fori_loop(0, slots, claim, 0)
+        return count + jnp.where(fresh, 1, 0)
+
+    count = lax.fori_loop(0, slots, claim, 0)
 
     def product(t, carry):
         for n in range(CAP):
@@ -469,22 +473,19 @@
     lax.fori_loop(0, bands, product, 0, unroll=8)
 
     def arrive(s, carry):
-        @pl.when(lead[s] == s)
-        def _():
-            for c in fetch(tags_s[s // CAP, s % CAP], s):
-                c.wait()
-        return carry
-
-    lax.fori_loop(0, slots, arrive, 0)
-
-    def add(s, carry):
-        @pl.when(lead[s] >= 0)
-        def _():
-            to = lead[s]
-            base[to] = base[to] + carried[s] * gate[to]
-        return carry
-
-    lax.fori_loop(0, slots, add, 0)
+        for c in fetch(0, 0):
+            c.wait()
+        return carry
+
+    lax.fori_loop(0, count, arrive, 0)
+
+    def add(t, carry):
+        for n in range(CAP):
+            to = lead[t * CAP + n]
+            base[to] = base[to] + carried[t * CAP + n] * gate[to]
+        return carry
+
+    lax.fori_loop(0, bands, add, 0)
 
     def send(s, carry):
         @pl.when(lead[s] == s)
@@ -492,14 +493,12 @@
             store(tags_s[s // CAP, s % CAP], s).start()
         return carry
 
-    def sent(s, carry):
-        @pl.when(lead[s] == s)
-        def _():
-            store(tags_s[s // CAP, s % CAP], s).wait()
+    def finish(s, carry):
+        store(0, 0).wait()
         return carry
 
     lax.fori_loop(0, slots, send, 0)
-    lax.fori_loop(0, slots, sent, 0)
+    lax.fori_loop(0, count, finish, 0)
 
 
 def smem():
@@ -546,9 +545,10 @@
 ):
     members, rows, cols = density.shape
     bands, flows = lax.axis_size("tile"), lax.axis_size("flow")
-    density, dispersal_draw, habitat_class, flow_tiles = (
+    flow_scale = flow_scale.reshape(1, -1)
+    density, dispersal_draw, habitat_class, flow_tiles, suitability, flow_scale, threshold = (
         pltpu.with_memory_space_constraint(x, pltpu.HBM)
-        for x in (density, dispersal_draw, habitat_class, flow_tiles))
+        for x in (density, dispersal_draw, habitat_class, flow_tiles, suitability, flow_scale, threshold))
     t, f = lax.axis_index("tile"), lax.axis_index("flow")
     place = jnp.stack([t % 2, f % 2, t, f]).astype(jnp.int32)
     hubs, share = hub_row.reshape(-1), jump_share.reshape(-1)
@@ -573,7 +573,7 @@
         ],
         compiler_params=params(24),
         name="edges",
-    )(place, density, habitat_class, suitability, flow_tiles, flow_scale.reshape(1, -1))
+    )(place, density, habitat_class, suitability, flow_tiles, flow_scale)
 
     got_a = lax.ppermute(cols_a, "flow", near_pairs(flows))
     got_b = lax.ppermute(cols_b, "flow", far_pairs(flows))
@@ -585,45 +585,16 @@
         compiler_params=params(24),
         name="corners",
     )(place, rows_a, rows_b, got_a, got_b)
+    rows_a, rows_b, tiles, dispersal_draw = lax.optimization_barrier((rows_a, rows_b, tiles, dispersal_draw))
     strip_a = lax.ppermute(rows_a, "tile", near_pairs(bands))
     strip_b = lax.ppermute(rows_b, "tile", far_pairs(bands))
 
-    stride = CAP * members + TAGS
-    sent, near, halo1, beside, coef, strips = pl.pallas_call(
-        hubs_kernel,
-        out_shape=(sds((bands * stride, cols), BF16), pack, pack, sds((4 * members, cols), F32),
-                   sds((rows + 16, cols), F32), sds((4, members, cols), F32)),
-        in_specs=[smem()] * 6 + [vmem()] * 7,
-        out_specs=(vmem(),) * 6,
-        scratch_shapes=[pltpu.SMEM((bands,), jnp.int32)],
-        compiler_params=params(24),
-        name="hubs",
-    )(place, hubs, dest_tile.reshape(-1), dest_row.reshape(-1), county_id.reshape(-1), share,
-      turned, weight, own, got_a, got_b, strip_a, strip_b)
-
-    landed = lax.all_to_all(sent, "tile", split_axis=0, concat_axis=0, tiled=True)
-    dispersal_draw, near = lax.optimization_barrier((dispersal_draw, near))
-    blocks = [tiles]
-    bit = flows // 2
-    offsets = [0]
-    while bit:
-        blocks += [lax.ppermute(x, "flow", [(i, i ^ bit) for i in range(flows)]) for x in blocks]
-        offsets += [o ^ bit for o in offsets]
-        bit //= 2
-    blocks = [x for _, x in sorted(zip(offsets, blocks), key=lambda p: p[0])]
-    table = pl.pallas_call(
-        table_kernel,
-        out_shape=sds((flows * per, depth + TAGS, cols), BF16),
-        in_specs=[smem()] + [vmem()] * flows,
-        out_specs=vmem(),
-        scratch_shapes=[pltpu.SemaphoreType.DMA],
-        compiler_params=params(24),
-        name="table",
-    )(place, *blocks)
+    def swap(x, bit):
+        return lax.ppermute(x, "flow", [(i, i ^ bit) for i in range(flows)])
 
     grow = pl.pallas_call(
         grow_kernel,
-        out_shape=sds(density.shape, F32),
+        out_shape=pltpu.HBM(density.shape, F32),
         in_specs=[hbm(), hbm()],
         out_specs=hbm(),
         scratch_shapes=[
@@ -639,6 +610,31 @@
     )(dispersal_draw, threshold)
     grow = pltpu.with_memory_space_constraint(grow, pltpu.HBM)
 
+    blocks = [tiles] + [None] * (flows - 1)
+    bits = [1 << k for k in reversed(range((flows - 1).bit_length()))]
+    for bit in bits:
+        blocks[bit] = swap(tiles, bit)
+    turned, grow, *early = lax.optimization_barrier([turned, grow] + [blocks[bit] for bit in bits])
+    for bit, x in zip(bits, early):
+        blocks[bit] = x
+    for d in range(flows):
+        if blocks[d] is None:
+            blocks[d] = swap(blocks[d & (d - 1)], d & -d)
+
+    stride = CAP * members + TAGS
+    sent, near, halo1, beside, coef, strips = pl.pallas_call(
+        hubs_kernel,
+        out_shape=(sds((bands * stride, cols), BF16), pack, pack, sds((4 * members, cols), F32),
+                   sds((rows + 16, cols), F32), sds((4, members, cols), F32)),
+        in_specs=[smem()] * 6 + [vmem()] * 7,
+        out_specs=(vmem(),) * 6,
+        scratch_shapes=[pltpu.SMEM((bands,), jnp.int32)],
+        compiler_params=params(24),
+        name="hubs",
+    )(place, hubs, dest_tile.reshape(-1), dest_row.reshape(-1), county_id.reshape(-1), share,
+      turned, weight, own, got_a, got_b, strip_a, strip_b)
+
+    landed = lax.all_to_all(sent, "tile", split_axis=0, concat_axis=0, tiled=True)
     kept = pl.pallas_call(
         bulk_kernel,
         out_shape=sds(density.shape, F32),
@@ -661,12 +657,13 @@
     out = pl.pallas_call(
         land_kernel,
         out_shape=sds(density.shape, F32),
-        in_specs=[vmem(), vmem(), hbm(), hbm()],
+        in_specs=[smem(), vmem(), hbm(), hbm()] + [vmem()] * flows,
         out_specs=hbm(),
         input_output_aliases={2: 0},
         scratch_shapes=[
-            pltpu.VMEM((slots, members, cols), F32),
-            pltpu.VMEM((slots, members, cols), F32),
+            pltpu.VMEM((flows * per, depth + TAGS, cols), BF16),
+            pltpu.VMEM((slots + 1, members, cols), F32),
+            pltpu.VMEM((slots + 1, members, cols), F32),
             pltpu.VMEM((slots, members, cols), F32),
             pltpu.VMEM((bands, cols), jnp.int32),
             pltpu.SMEM((bands, cols), jnp.int32),
@@ -678,7 +675,7 @@
         ],
         compiler_params=params(24),
         name="land",
-    )(landed, table, kept, grow)
+    )(place, landed, kept, grow, *blocks)
     return out
 
 

time: 54.5 us -> 49.4 us (0.906)
  the two profiles are of different devices: /device:TPU:1 before, /device:TPU:0 now
where the time goes in v2:
time: 49.4 us; the launch traced here: 48.9 us
  Pallas kernels  23.8 us (48%)
  starting transfers between devices  18.8 us (38%)
  waiting for transfers between devices  6 us (12%)
    pallas_call x1, Pallas kernels, local(): pl.pallas_call(bulk_kernel, out_shape=sds(density.shape, F32), in_specs=[...  8.71 us
    all_to_all x1, starting transfers between devices, local(): lax.all_to_all(sent, 'tile', split_axis=0, concat_axis=0, tiled=True)  8.11 us
    ppermute x3, starting transfers between devices, swap(): return lax.ppermute(x, 'flow', [(i, i ^ bit) for i in range(flows)])  7.36 us
    all_to_all x1, waiting for transfers between devices, local(): lax.all_to_all(sent, 'tile', split_axis=0, concat_axis=0, tiled=True)  5.74 us
    pallas_call x1, Pallas kernels, local(): pl.pallas_call(land_kernel, out_shape=sds(density.shape, F32), in_specs=[...  3.99 us
    pallas_call x1, Pallas kernels, local(): pl.pallas_call(edges_kernel, out_shape=(message, message, message, messag...  3.76 us
    pallas_call x1, Pallas kernels, local(): pl.pallas_call(hubs_kernel, out_shape=(sds((bands * stride, cols), BF16),...  3.58 us
    pallas_call x1, Pallas kernels, local(): pl.pallas_call(grow_kernel, out_shape=pltpu.HBM(density.shape, F32), in_s...  3.13 us
  transfers between devices with their start and end apart: 8, of which 2 were waited for; matrix products, arithmetic and copies ran while one was open for 0% of the time, Pallas kernels for 24%

profile of v2, /device:TPU:0, one launch (start us, length us, event | category | flops | bytes accessed | tf_op | source)
XLA Modules:
  0.0 48.9 jit_solution(15548070349140933272)
XLA Ops:
  0.0 0.1 pad_add_fusion.place
  0.1 3.8 %edges.1 = (f32[136,128]{1,0:T(8,128)S(1)}, f32[136,128]{1,0:T(8,128)S(1)}, f32[136,128]{1,0:T(8,128)S(1)}, f32[136,128]{1,0:T(8,128)S(1)}, f32[128,128]{1,0:T(8...) custom-call(s32[4]{0:T(128)S(1)} %pad_add_fusion.place, ...), custom_call_target="tpu_custom_call" | custom-call | tf_op jit(solution)/shard_map/edges/pallas_call | solution.py:559
  3.8 0.0 copy-start
  3.9 0.0 copy-start.1
  3.9 0.0 copy-start.2
  3.9 0.0 copy-start.3
  3.9 0.0 copy-start.4
  3.9 0.5 %collective-permute-start = (f32[136,128]{1,0:T(8,128)S(1)}, f32[136,128]{1,0:T(8,128)S(1)}, u32[]{:S(2)}, u32[]{:S(2)}) collective-permute-start(f32[136,128]{1,0:T(8,128)S(1)} %get-tuple-element.32), channel_id=1, source_target_pairs={{0,1},{1,0},{2,3},{3,2},{4,5},{5,4},{6,7},{7,6},{8,9},{9,8},{10,11... | collective-permute-start | bytes 208904 | tf_op jit(solution)/shard_map/ppermute | solution.py:578
  4.4 0.7 %collective-permute-start.1 = (f32[136,128]{1,0:T(8,128)S(1)}, f32[136,128]{1,0:T(8,128)S(1)}, u32[]{:S(2)}, u32[]{:S(2)}) collective-permute-start(f32[136,128]{1,0:T(8,128)S(1)} %get-tuple-element.33), channel_id=1, source_target_pairs={{1,2},{2,1},{5,6},{6,5},{9,10},{10,9},{13,14},{14,13},{17,18},{18,... | collective-permute-start | bytes 208904 | tf_op jit(solution)/shard_map/ppermute | solution.py:579
  5.1 0.2 collective-permute-done.got_a.cols_a
  5.3 0.7 %corners.1 = (f32[136,128]{1,0:T(8,128)S(1)}, f32[136,128]{1,0:T(8,128)S(1)}) custom-call(s32[4]{0:T(128)S(1)} %pad_add_fusion.place, f32[136,128]{1,0:T(8,128)S(1)} %get-tuple-element.30.rows_a, f32[136,128]{1,0:T(8,128)S(1)} %get-tuple-element.31.rows_b, f32[136,128]{1,0:T(8,128)S(1)} %collective-permute-done.got_a.cols_a, ...), custom_call_target="tpu_custom_call" | custom-call | tf_op jit(solution)/shard_map/corners/pallas_call | solution.py:580
  6.0 5.7 %collective-permute-start.3 = (bf16[4,144,128]{2,1,0:T(8,128)(2,1)S(1)}, bf16[4,144,128]{2,1,0:T(8,128)(2,1)S(1)}, u32[]{:S(2)}, u32[]{:S(2)}) collective-permute-start(bf16[4,144,128]{2,1,0:T(8,128)(2,1)S(1)} %get-tuple-element.38.rest_0_), channel_id=1, source_target_pairs={{0,1},{1,0},{2,3},{3,2},{4,5},{5,4},{6,7},{7,6},{8,9},{9,8},{10,11... | collective-permute-start | bytes 442376 | tf_op jit(solution)/shard_map/ppermute | solution.py:593
  11.7 1.7 %collective-permute-start.2 = (bf16[4,144,128]{2,1,0:T(8,128)(2,1)S(1)}, bf16[4,144,128]{2,1,0:T(8,128)(2,1)S(1)}, u32[]{:S(2)}, u32[]{:S(2)}) collective-permute-start(bf16[4,144,128]{2,1,0:T(8,128)(2,1)S(1)} %get-tuple-element.38.rest_0_), channel_id=1, source_target_pairs={{0,2},{1,3},{2,0},{3,1},{4,6},{5,7},{6,4},{7,5},{8,10},{9,11},{10,... | collective-permute-start | bytes 442376 | tf_op jit(solution)/shard_map/ppermute | solution.py:593
  13.4 1.5 %collective-permute-start.4 = (f32[136,128]{1,0:T(8,128)S(1)}, f32[136,128]{1,0:T(8,128)S(1)}, u32[]{:S(2)}, u32[]{:S(2)}) collective-permute-start(f32[136,128]{1,0:T(8,128)S(1)} %get-tuple-element.42), channel_id=1, source_target_pairs={{0,4},{4,0},{8,12},{12,8},{16,20},{20,16},{24,28},{28,24},{1,5},{5... | collective-permute-start | bytes 208904 | tf_op jit(solution)/shard_map/ppermute | solution.py:589
  14.9 0.7 %collective-permute-start.5 = (f32[136,128]{1,0:T(8,128)S(1)}, f32[136,128]{1,0:T(8,128)S(1)}, u32[]{:S(2)}, u32[]{:S(2)}) collective-permute-start(f32[136,128]{1,0:T(8,128)S(1)} %get-tuple-element.43), channel_id=1, source_target_pairs={{4,8},{8,4},{12,16},{16,12},{20,24},{24,20},{5,9},{9,5},{13,17},{1... | collective-permute-start | bytes 208904 | tf_op jit(solution)/shard_map/ppermute | solution.py:590
  15.5 3.1 %grow.1 = f32[64,128,128]{2,1,0:T(8,128)} custom-call(bf16[64,128,128]{2,1,0:T(8,128)(2,1)} %draw, f32[128,128]{1,0:T(8,128)} %threshold.1), custom_call_target="tpu_custom_call" | custom-call | tf_op jit(solution)/shard_map/grow/pallas_call | solution.py:595
  18.7 0.0 collective-permute-done.2.rest_2_
  18.7 0.0 collective-permute-done.4.rows_a
  18.8 3.6 %hubs.1 = (bf16[2176,128]{1,0:T(8,128)(2,1)}, f32[128,128]{1,0:T(8,128)S(1)}, f32[128,128]{1,0:T(8,128)S(1)}, f32[256,128]{1,0:T(8,128)S(1)}, f32[144,128]{1,0:T(8,128)S(1)}, /*index=5*/f32[4,64,128]{2,1,0:T(8,128)S(1)}) custom-call(s32[4]{0:T(128)S(1)} %pad_add_fusion.place, s32[16]{0:T(128)S(1)} %bitcast.13, s32[16]{0:T(128)S(1)} %bitcast.17, ...), custom_call_target="tpu_custom_call" | custom-call | tf_op jit(solution)/shard_map/hubs/pallas_call | solution.py:625
  22.4 8.1 %all-to-all-start = ((bf16[8,272,128]{2,1,0:T(8,128)(2,1)}), bf16[8,272,128]{2,1,0:T(8,128)(2,1)S(1)}, u32[]{:S(2)}, u32[]{:S(2)}) async-start(bf16[8,272,128]{2,1,0:T(8,128)(2,1)} %bitcast.10), calls=%async_computation | async-start | bytes 1114112 | tf_op jit(solution)/shard_map/all_to_all | solution.py:637
  30.5 0.0 collective-permute-start.6
  30.5 8.7 %bulk.1.kept = f32[64,128,128]{2,1,0:T(8,128)} custom-call(s32[16]{0:T(128)S(1)} %bitcast.14, f32[16]{0:T(128)S(1)} %bitcast.16, f32[64,128,128]{2,1,0:T(8,128)} %density.3, f32[64,128,128]{2,1,0:T(8,128)} %grow.1, f32[144,128]{1,0:T(8,128)S(1)} %get-tuple-element.46.coef, f32[4,64,128]{2,1,0:T(8,128)S(1)} %get-tuple-element.47.strips, ...), custom_call_target="tpu_custom_call" | custom-call | tf_op jit(solution)/shard_map/bulk/pallas_call | solution.py:638
  39.2 5.7 %all-to-all-done = bf16[8,272,128]{2,1,0:T(8,128)(2,1)S(1)} async-done(((bf16[8,272,128]{2,1,0:T(8,128)(2,1)}), bf16[8,272,128]{2,1,0:T(8,128)(2,1)S(1)}, u32[]{:S(2)}, u32[]{:S(2)}) %all-to-all-start) | async-done | bytes 557088 | tf_op jit(solution)/shard_map/all_to_all | solution.py:637
  44.9 4.0 %land.1 = f32[64,128,128]{2,1,0:T(8,128)} custom-call(s32[4]{0:T(128)S(1)} %pad_add_fusion.place, bf16[2176,128]{1,0:T(8,128)(2,1)S(1)} %bitcast.12, f32[64,128,128]{2,1,0:T(8,128)} %bulk.1.kept, f32[64,128,128]{2,1,0:T(8,128)} %grow.1, bf16[4,144,128]{2,1,0:T(8,128)(2,1)S(1)} %get-tuple-element.38.rest_0_, ...), custom_call_target="tpu_custom_call", output_to_operand_aliasing={{}: (2, {})} | custom-call | tf_op jit(solution)/shard_map/land/pallas_call | solution.py:657
  (9 shorter events, 0.0 us)
Async XLA Ops:
  3.8 14.9 %copy-start = (s32[1,16]{1,0:T(1,128)S(1)}, s32[1,16]{1,0:T(1,128)}, u32[]{:S(2)}) copy-start(s32[1,16]{1,0:T(1,128)} %param.17) | copy-start | bytes 196
  3.9 14.9 %copy-start.1 = (f32[1,16]{1,0:T(1,128)S(1)}, f32[1,16]{1,0:T(1,128)}, u32[]{:S(2)}) copy-start(f32[1,16]{1,0:T(1,128)} %param.21) | copy-start | bytes 196
  3.9 14.9 %copy-start.2 = (s32[1,16,1]{1,2,0:T(1,128)S(1)}, s32[1,16,1]{1,2,0:T(1,128)}, u32[]{:S(2)}) copy-start(s32[1,16,1]{1,2,0:T(1,128)} %param.18) | copy-start | bytes 196
  3.9 14.9 %copy-start.3 = (s32[1,16]{1,0:T(1,128)S(1)}, s32[1,16]{1,0:T(1,128)}, u32[]{:S(2)}) copy-start(s32[1,16]{1,0:T(1,128)} %param.19) | copy-start | bytes 196
  3.9 14.9 %copy-start.4 = (s32[1,16]{1,0:T(1,128)S(1)}, s32[1,16]{1,0:T(1,128)}, u32[]{:S(2)}) copy-start(s32[1,16]{1,0:T(1,128)} %param.20) | copy-start | bytes 196
  3.9 1.4 %collective-permute-start = (f32[136,128]{1,0:T(8,128)S(1)}, f32[136,128]{1,0:T(8,128)S(1)}, u32[]{:S(2)}, u32[]{:S(2)}) collective-permute-start(f32[136,128]{1,0:T(8,128)S(1)} %get-tuple-element.32), channel_id=1, source_target_pairs={{0,1},{1,0},{2,3},{3,2},{4,5},{5,4},{6,7},{7,6},{8,9},{9,8},{10,11... | collective-permute-start | bytes 208904 | tf_op jit(solution)/shard_map/ppermute | solution.py:578
  4.4 0.9 %collective-permute-start.1 = (f32[136,128]{1,0:T(8,128)S(1)}, f32[136,128]{1,0:T(8,128)S(1)}, u32[]{:S(2)}, u32[]{:S(2)}) collective-permute-start(f32[136,128]{1,0:T(8,128)S(1)} %get-tuple-element.33), channel_id=1, source_target_pairs={{1,2},{2,1},{5,6},{6,5},{9,10},{10,9},{13,14},{14,13},{17,18},{18,... | collective-permute-start | bytes 208904 | tf_op jit(solution)/shard_map/ppermute | solution.py:579
  6.0 12.7 %collective-permute-start.3 = (bf16[4,144,128]{2,1,0:T(8,128)(2,1)S(1)}, bf16[4,144,128]{2,1,0:T(8,128)(2,1)S(1)}, u32[]{:S(2)}, u32[]{:S(2)}) collective-permute-start(bf16[4,144,128]{2,1,0:T(8,128)(2,1)S(1)} %get-tuple-element.38.rest_0_), channel_id=1, source_target_pairs={{0,1},{1,0},{2,3},{3,2},{4,5},{5,4},{6,7},{7,6},{8,9},{9,8},{10,11... | collective-permute-start | bytes 442376 | tf_op jit(solution)/shard_map/ppermute | solution.py:593
  11.7 7.0 %collective-permute-start.2 = (bf16[4,144,128]{2,1,0:T(8,128)(2,1)S(1)}, bf16[4,144,128]{2,1,0:T(8,128)(2,1)S(1)}, u32[]{:S(2)}, u32[]{:S(2)}) collective-permute-start(bf16[4,144,128]{2,1,0:T(8,128)(2,1)S(1)} %get-tuple-element.38.rest_0_), channel_id=1, source_target_pairs={{0,2},{1,3},{2,0},{3,1},{4,6},{5,7},{6,4},{7,5},{8,10},{9,11},{10,... | collective-permute-start | bytes 442376 | tf_op jit(solution)/shard_map/ppermute | solution.py:593
  13.4 5.3 %collective-permute-start.4 = (f32[136,128]{1,0:T(8,128)S(1)}, f32[136,128]{1,0:T(8,128)S(1)}, u32[]{:S(2)}, u32[]{:S(2)}) collective-permute-start(f32[136,128]{1,0:T(8,128)S(1)} %get-tuple-element.42), channel_id=1, source_target_pairs={{0,4},{4,0},{8,12},{12,8},{16,20},{20,16},{24,28},{28,24},{1,5},{5... | collective-permute-start | bytes 208904 | tf_op jit(solution)/shard_map/ppermute | solution.py:589
  14.9 3.8 %collective-permute-start.5 = (f32[136,128]{1,0:T(8,128)S(1)}, f32[136,128]{1,0:T(8,128)S(1)}, u32[]{:S(2)}, u32[]{:S(2)}) collective-permute-start(f32[136,128]{1,0:T(8,128)S(1)} %get-tuple-element.43), channel_id=1, source_target_pairs={{4,8},{8,4},{12,16},{16,12},{20,24},{24,20},{5,9},{9,5},{13,17},{1... | collective-permute-start | bytes 208904 | tf_op jit(solution)/shard_map/ppermute | solution.py:590
  22.4 22.6 %all-to-all-start = ((bf16[8,272,128]{2,1,0:T(8,128)(2,1)}), bf16[8,272,128]{2,1,0:T(8,128)(2,1)S(1)}, u32[]{:S(2)}, u32[]{:S(2)}) async-start(bf16[8,272,128]{2,1,0:T(8,128)(2,1)} %bitcast.10), calls=%async_computation | async-start | bytes 1114112 | tf_op jit(solution)/shard_map/all_to_all | solution.py:637
  30.5 8.7 %collective-permute-start.6 = (bf16[4,144,128]{2,1,0:T(8,128)(2,1)S(1)}, bf16[4,144,128]{2,1,0:T(8,128)(2,1)S(1)}, u32[]{:S(2)}, u32[]{:S(2)}) collective-permute-start(bf16[4,144,128]{2,1,0:T(8,128)(2,1)S(1)} %collective-permute-done.2.rest_2_), channel_id=1, source_target_pairs={{0,1},{1,0},{2,3},{3,2},{4,5},{5,4},{6,7},{7,6},{8,9},{9,8},{10,11... | collective-permute-start | bytes 442376 | tf_op jit(solution)/shard_map/ppermute | solution.py:593

commit v3 on v2

--- a/solution.py
+++ b/solution.py
@@ -11,7 +11,7 @@
 TAIL = 8
 TAGS = 16
 CHUNK = 16
-UNROLL = 4
+UNROLL = 8
 STEP = 16
 GROW = 16
 MIB = 1024 * 1024
@@ -234,12 +234,13 @@
     edge = jnp.logical_or(first, last)
     band = (cols, cols)
     mask = (jnp.abs(lanes(band) - sublanes(band)) == 1).astype(BF16)
+    mask = jnp.concatenate([mask, mask], axis=0)
 
     def lateral(rows_in):
         flat = jnp.concatenate(rows_in, axis=0)
         high = flat.astype(BF16)
         low = (flat - high.astype(F32)).astype(BF16)
-        both = jnp.dot(high, mask, preferred_element_type=F32) + jnp.dot(low, mask, preferred_element_type=F32)
+        both = jnp.dot(jnp.concatenate([high, low], axis=1), mask, preferred_element_type=F32)
         return [both[k * members:(k + 1) * members] for k in range(len(rows_in))]
 
     def relax(c, n, s, h, w, across):
@@ -351,13 +352,14 @@
     edge = jnp.logical_or(first, last)
     band = (cols, cols)
     beside_mask = (jnp.abs(lanes(band) - sublanes(band)) == 1).astype(BF16)
+    beside_mask = jnp.concatenate([beside_mask, beside_mask], axis=0)
 
     def lateral(c):
         flat = c.reshape(-1, cols)
         high = flat.astype(BF16)
         low = (flat - high.astype(F32)).astype(BF16)
-        both = jnp.dot(high, beside_mask, preferred_element_type=F32)
-        return (both + jnp.dot(low, beside_mask, preferred_element_type=F32)).reshape(c.shape)
+        parts = jnp.concatenate([high, low], axis=1)
+        return jnp.dot(parts, beside_mask, preferred_element_type=F32).reshape(c.shape)
 
     def relax(c, n, s, h, w, across):
         return c + w * ((n + s) + (across + jnp.where(edge, h, 0.0)) - 4.0 * c)
@@ -585,7 +587,7 @@
         compiler_params=params(24),
         name="corners",
     )(place, rows_a, rows_b, got_a, got_b)
-    rows_a, rows_b, tiles, dispersal_draw = lax.optimization_barrier((rows_a, rows_b, tiles, dispersal_draw))
+    rows_a, rows_b, dispersal_draw = lax.optimization_barrier((rows_a, rows_b, dispersal_draw))
     strip_a = lax.ppermute(rows_a, "tile", near_pairs(bands))
     strip_b = lax.ppermute(rows_b, "tile", far_pairs(bands))
 
@@ -610,16 +612,8 @@
     )(dispersal_draw, threshold)
     grow = pltpu.with_memory_space_constraint(grow, pltpu.HBM)
 
-    blocks = [tiles] + [None] * (flows - 1)
-    bits = [1 << k for k in reversed(range((flows - 1).bit_length()))]
-    for bit in bits:
-        blocks[bit] = swap(tiles, bit)
-    turned, grow, *early = lax.optimization_barrier([turned, grow] + [blocks[bit] for bit in bits])
-    for bit, x in zip(bits, early):
-        blocks[bit] = x
-    for d in range(flows):
-        if blocks[d] is None:
-            blocks[d] = swap(blocks[d & (d - 1)], d & -d)
+    blocks = [tiles] + [swap(tiles, d) for d in range(1, flows)]
+    turned, grow = lax.optimization_barrier((turned, grow))
 
     stride = CAP * members + TAGS
     sent, near, halo1, beside, coef, strips = pl.pallas_call(

time: 49.4 us -> 44.8 us (0.907)
  the two profiles are of different devices: /device:TPU:0 before, /device:TPU:1 now
where the time goes in v3:
time: 44.8 us; the launch traced here: 44.2 us
  Pallas kernels  23.2 us (52%)
  starting transfers between devices  16.9 us (38%)
  waiting for transfers between devices  3.85 us (9%)
    pallas_call x1, Pallas kernels, local(): pl.pallas_call(bulk_kernel, out_shape=sds(density.shape, F32), in_specs=[...  8.47 us
    all_to_all x1, starting transfers between devices, local(): lax.all_to_all(sent, 'tile', split_axis=0, concat_axis=0, tiled=True)  7.03 us
    ppermute x1, starting transfers between devices, local(): got_b = lax.ppermute(cols_b, 'flow', far_pairs(flows))  4.47 us
    pallas_call x1, Pallas kernels, local(): pl.pallas_call(land_kernel, out_shape=sds(density.shape, F32), in_specs=[...  3.94 us
    pallas_call x1, Pallas kernels, local(): pl.pallas_call(edges_kernel, out_shape=(message, message, message, messag...  3.76 us
    pallas_call x1, Pallas kernels, local(): pl.pallas_call(hubs_kernel, out_shape=(sds((bands * stride, cols), BF16),...  3.19 us
    pallas_call x1, Pallas kernels, local(): pl.pallas_call(grow_kernel, out_shape=pltpu.HBM(density.shape, F32), in_s...  3.13 us
    ppermute x3, starting transfers between devices, swap(): return lax.ppermute(x, 'flow', [(i, i ^ bit) for i in range(flows)])  2.68 us
  transfers between devices with their start and end apart: 8, of which 2 were waited for; matrix products, arithmetic and copies ran while one was open for 0% of the time, Pallas kernels for 26%

profile of v3, /device:TPU:1, one launch (start us, length us, event | category | flops | bytes accessed | tf_op | source)
XLA Modules:
  0.0 44.2 jit_solution(8331727738256417359)
XLA Ops:
  0.0 0.1 pad_add_fusion.place
  0.1 3.8 %edges.1 = (f32[136,128]{1,0:T(8,128)S(1)}, f32[136,128]{1,0:T(8,128)S(1)}, f32[136,128]{1,0:T(8,128)S(1)}, f32[136,128]{1,0:T(8,128)S(1)}, f32[128,128]{1,0:T(8...) custom-call(s32[4]{0:T(128)S(1)} %pad_add_fusion.place, ...), custom_call_target="tpu_custom_call" | custom-call | tf_op jit(solution)/shard_map/edges/pallas_call | solution.py:561
  3.8 0.0 copy-start
  3.9 0.0 copy-start.1
  3.9 0.0 copy-start.2
  3.9 0.0 copy-start.3
  3.9 0.0 copy-start.4
  3.9 0.1 collective-permute-start
  4.0 4.5 %collective-permute-start.1 = (f32[136,128]{1,0:T(8,128)S(1)}, f32[136,128]{1,0:T(8,128)S(1)}, u32[]{:S(2)}, u32[]{:S(2)}) collective-permute-start(f32[136,128]{1,0:T(8,128)S(1)} %get-tuple-element.30), channel_id=1, source_target_pairs={{1,2},{2,1},{5,6},{6,5},{9,10},{10,9},{13,14},{14,13},{17,18},{18,... | collective-permute-start | bytes 208904 | tf_op jit(solution)/shard_map/ppermute | solution.py:581
  8.5 0.0 collective-permute-done.got_a.cols_a
  8.5 2.3 %collective-permute-done.1.got_b.cols_b = f32[136,128]{1,0:T(8,128)S(1)} collective-permute-done((f32[136,128]{1,0:T(8,128)S(1)}, f32[136,128]{1,0:T(8,128)S(1)}, u32[]{:S(2)}, u32[]{:S(2)}) %collective-permute-start.1) | collective-permute-done | bytes 69664 | tf_op jit(solution)/shard_map/ppermute | solution.py:581
  10.8 0.7 %corners.1 = (f32[136,128]{1,0:T(8,128)S(1)}, f32[136,128]{1,0:T(8,128)S(1)}) custom-call(s32[4]{0:T(128)S(1)} %pad_add_fusion.place, f32[136,128]{1,0:T(8,128)S(1)} %get-tuple-element.27.rows_a, f32[136,128]{1,0:T(8,128)S(1)} %get-tuple-element.28.rows_b, f32[136,128]{1,0:T(8,128)S(1)} %collective-permute-done.got_a.cols_a, ...), custom_call_target="tpu_custom_call" | custom-call | tf_op jit(solution)/shard_map/corners/pallas_call | solution.py:582
  11.4 1.9 %collective-permute-start.2 = (f32[136,128]{1,0:T(8,128)S(1)}, f32[136,128]{1,0:T(8,128)S(1)}, u32[]{:S(2)}, u32[]{:S(2)}) collective-permute-start(f32[136,128]{1,0:T(8,128)S(1)} %get-tuple-element.37), channel_id=1, source_target_pairs={{0,4},{4,0},{8,12},{12,8},{16,20},{20,16},{24,28},{28,24},{1,5},{5... | collective-permute-start | bytes 208904 | tf_op jit(solution)/shard_map/ppermute | solution.py:591
  13.4 0.7 %collective-permute-start.3 = (f32[136,128]{1,0:T(8,128)S(1)}, f32[136,128]{1,0:T(8,128)S(1)}, u32[]{:S(2)}, u32[]{:S(2)}) collective-permute-start(f32[136,128]{1,0:T(8,128)S(1)} %get-tuple-element.38), channel_id=1, source_target_pairs={{4,8},{8,4},{12,16},{16,12},{20,24},{24,20},{5,9},{9,5},{13,17},{1... | collective-permute-start | bytes 208904 | tf_op jit(solution)/shard_map/ppermute | solution.py:592
  14.0 3.1 %grow.1 = f32[64,128,128]{2,1,0:T(8,128)} custom-call(bf16[64,128,128]{2,1,0:T(8,128)(2,1)} %draw, f32[128,128]{1,0:T(8,128)} %threshold.1), custom_call_target="tpu_custom_call" | custom-call | tf_op jit(solution)/shard_map/grow/pallas_call | solution.py:597
  17.2 0.0 collective-permute-done.2.rows_a
  17.2 0.0 collective-permute-done.3.rows_b
  17.2 3.2 %hubs.1 = (bf16[2176,128]{1,0:T(8,128)(2,1)}, f32[128,128]{1,0:T(8,128)S(1)}, f32[128,128]{1,0:T(8,128)S(1)}, f32[256,128]{1,0:T(8,128)S(1)}, f32[144,128]{1,0:T(8,128)S(1)}, /*index=5*/f32[4,64,128]{2,1,0:T(8,128)S(1)}) custom-call(s32[4]{0:T(128)S(1)} %pad_add_fusion.place, s32[16]{0:T(128)S(1)} %bitcast.13, s32[16]{0:T(128)S(1)} %bitcast.17, ...), custom_call_target="tpu_custom_call" | custom-call | tf_op jit(solution)/shard_map/hubs/pallas_call | solution.py:619
  20.4 7.0 %all-to-all-start = ((bf16[8,272,128]{2,1,0:T(8,128)(2,1)}), bf16[8,272,128]{2,1,0:T(8,128)(2,1)S(1)}, u32[]{:S(2)}, u32[]{:S(2)}) async-start(bf16[8,272,128]{2,1,0:T(8,128)(2,1)} %bitcast.10), calls=%async_computation | async-start | bytes 1114112 | tf_op jit(solution)/shard_map/all_to_all | solution.py:631
  27.5 2.2 %collective-permute-start.6 = (bf16[4,144,128]{2,1,0:T(8,128)(2,1)S(1)}, bf16[4,144,128]{2,1,0:T(8,128)(2,1)S(1)}, u32[]{:S(2)}, u32[]{:S(2)}) collective-permute-start(bf16[4,144,128]{2,1,0:T(8,128)(2,1)S(1)} %get-tuple-element.46.rest_0_), channel_id=1, source_target_pairs={{0,3},{1,2},{2,1},{3,0},{4,7},{5,6},{6,5},{7,4},{8,11},{9,10},{10,... | collective-permute-start | bytes 442376 | tf_op jit(solution)/shard_map/ppermute | solution.py:595
  29.7 0.5 %collective-permute-start.4 = (bf16[4,144,128]{2,1,0:T(8,128)(2,1)S(1)}, bf16[4,144,128]{2,1,0:T(8,128)(2,1)S(1)}, u32[]{:S(2)}, u32[]{:S(2)}) collective-permute-start(bf16[4,144,128]{2,1,0:T(8,128)(2,1)S(1)} %get-tuple-element.46.rest_0_), channel_id=1, source_target_pairs={{0,1},{1,0},{2,3},{3,2},{4,5},{5,4},{6,7},{7,6},{8,9},{9,8},{10,11... | collective-permute-start | bytes 442376 | tf_op jit(solution)/shard_map/ppermute | solution.py:595
  30.1 8.5 %bulk.1.kept = f32[64,128,128]{2,1,0:T(8,128)} custom-call(s32[16]{0:T(128)S(1)} %bitcast.14, f32[16]{0:T(128)S(1)} %bitcast.16, f32[64,128,128]{2,1,0:T(8,128)} %density.3, f32[64,128,128]{2,1,0:T(8,128)} %grow.1, f32[144,128]{1,0:T(8,128)S(1)} %get-tuple-element.41.coef, f32[4,64,128]{2,1,0:T(8,128)S(1)} %get-tuple-element.42.strips, ...), custom_call_target="tpu_custom_call" | custom-call | tf_op jit(solution)/shard_map/bulk/pallas_call | solution.py:632
  38.6 1.6 %all-to-all-done = bf16[8,272,128]{2,1,0:T(8,128)(2,1)S(1)} async-done(((bf16[8,272,128]{2,1,0:T(8,128)(2,1)}), bf16[8,272,128]{2,1,0:T(8,128)(2,1)S(1)}, u32[]{:S(2)}, u32[]{:S(2)}) %all-to-all-start) | async-done | bytes 557088 | tf_op jit(solution)/shard_map/all_to_all | solution.py:631
  40.2 3.9 %land.1 = f32[64,128,128]{2,1,0:T(8,128)} custom-call(s32[4]{0:T(128)S(1)} %pad_add_fusion.place, bf16[2176,128]{1,0:T(8,128)(2,1)S(1)} %bitcast.12, f32[64,128,128]{2,1,0:T(8,128)} %bulk.1.kept, f32[64,128,128]{2,1,0:T(8,128)} %grow.1, bf16[4,144,128]{2,1,0:T(8,128)(2,1)S(1)} %get-tuple-element.46.rest_0_, ...), custom_call_target="tpu_custom_call", output_to_operand_aliasing={{}: (2, {})} | custom-call | tf_op jit(solution)/shard_map/land/pallas_call | solution.py:651
  (9 shorter events, 0.0 us)
Async XLA Ops:
  3.8 13.3 %copy-start = (s32[1,16]{1,0:T(1,128)S(1)}, s32[1,16]{1,0:T(1,128)}, u32[]{:S(2)}) copy-start(s32[1,16]{1,0:T(1,128)} %param.17) | copy-start | bytes 196
  3.9 13.3 %copy-start.1 = (f32[1,16]{1,0:T(1,128)S(1)}, f32[1,16]{1,0:T(1,128)}, u32[]{:S(2)}) copy-start(f32[1,16]{1,0:T(1,128)} %param.21) | copy-start | bytes 196
  3.9 13.3 %copy-start.2 = (s32[1,16,1]{1,2,0:T(1,128)S(1)}, s32[1,16,1]{1,2,0:T(1,128)}, u32[]{:S(2)}) copy-start(s32[1,16,1]{1,2,0:T(1,128)} %param.18) | copy-start | bytes 196
  3.9 13.3 %copy-start.3 = (s32[1,16]{1,0:T(1,128)S(1)}, s32[1,16]{1,0:T(1,128)}, u32[]{:S(2)}) copy-start(s32[1,16]{1,0:T(1,128)} %param.19) | copy-start | bytes 196
  3.9 13.3 %copy-start.4 = (s32[1,16]{1,0:T(1,128)S(1)}, s32[1,16]{1,0:T(1,128)}, u32[]{:S(2)}) copy-start(s32[1,16]{1,0:T(1,128)} %param.20) | copy-start | bytes 196
  3.9 4.6 %collective-permute-start = (f32[136,128]{1,0:T(8,128)S(1)}, f32[136,128]{1,0:T(8,128)S(1)}, u32[]{:S(2)}, u32[]{:S(2)}) collective-permute-start(f32[136,128]{1,0:T(8,128)S(1)} %get-tuple-element.29), channel_id=1, source_target_pairs={{0,1},{1,0},{2,3},{3,2},{4,5},{5,4},{6,7},{7,6},{8,9},{9,8},{10,11... | collective-permute-start | bytes 208904 | tf_op jit(solution)/shard_map/ppermute | solution.py:580
  4.0 6.7 %collective-permute-start.1 = (f32[136,128]{1,0:T(8,128)S(1)}, f32[136,128]{1,0:T(8,128)S(1)}, u32[]{:S(2)}, u32[]{:S(2)}) collective-permute-start(f32[136,128]{1,0:T(8,128)S(1)} %get-tuple-element.30), channel_id=1, source_target_pairs={{1,2},{2,1},{5,6},{6,5},{9,10},{10,9},{13,14},{14,13},{17,18},{18,... | collective-permute-start | bytes 208904 | tf_op jit(solution)/shard_map/ppermute | solution.py:581
  11.4 5.7 %collective-permute-start.2 = (f32[136,128]{1,0:T(8,128)S(1)}, f32[136,128]{1,0:T(8,128)S(1)}, u32[]{:S(2)}, u32[]{:S(2)}) collective-permute-start(f32[136,128]{1,0:T(8,128)S(1)} %get-tuple-element.37), channel_id=1, source_target_pairs={{0,4},{4,0},{8,12},{12,8},{16,20},{20,16},{24,28},{28,24},{1,5},{5... | collective-permute-start | bytes 208904 | tf_op jit(solution)/shard_map/ppermute | solution.py:591
  13.4 3.8 %collective-permute-start.3 = (f32[136,128]{1,0:T(8,128)S(1)}, f32[136,128]{1,0:T(8,128)S(1)}, u32[]{:S(2)}, u32[]{:S(2)}) collective-permute-start(f32[136,128]{1,0:T(8,128)S(1)} %get-tuple-element.38), channel_id=1, source_target_pairs={{4,8},{8,4},{12,16},{16,12},{20,24},{24,20},{5,9},{9,5},{13,17},{1... | collective-permute-start | bytes 208904 | tf_op jit(solution)/shard_map/ppermute | solution.py:592
  20.4 19.8 %all-to-all-start = ((bf16[8,272,128]{2,1,0:T(8,128)(2,1)}), bf16[8,272,128]{2,1,0:T(8,128)(2,1)S(1)}, u32[]{:S(2)}, u32[]{:S(2)}) async-start(bf16[8,272,128]{2,1,0:T(8,128)(2,1)} %bitcast.10), calls=%async_computation | async-start | bytes 1114112 | tf_op jit(solution)/shard_map/all_to_all | solution.py:631
  27.5 11.2 %collective-permute-start.6 = (bf16[4,144,128]{2,1,0:T(8,128)(2,1)S(1)}, bf16[4,144,128]{2,1,0:T(8,128)(2,1)S(1)}, u32[]{:S(2)}, u32[]{:S(2)}) collective-permute-start(bf16[4,144,128]{2,1,0:T(8,128)(2,1)S(1)} %get-tuple-element.46.rest_0_), channel_id=1, source_target_pairs={{0,3},{1,2},{2,1},{3,0},{4,7},{5,6},{6,5},{7,4},{8,11},{9,10},{10,... | collective-permute-start | bytes 442376 | tf_op jit(solution)/shard_map/ppermute | solution.py:595
  29.7 9.0 %collective-permute-start.5 = (bf16[4,144,128]{2,1,0:T(8,128)(2,1)S(1)}, bf16[4,144,128]{2,1,0:T(8,128)(2,1)S(1)}, u32[]{:S(2)}, u32[]{:S(2)}) collective-permute-start(bf16[4,144,128]{2,1,0:T(8,128)(2,1)S(1)} %get-tuple-element.46.rest_0_), channel_id=1, source_target_pairs={{0,2},{1,3},{2,0},{3,1},{4,6},{5,7},{6,4},{7,5},{8,10},{9,11},{10,... | collective-permute-start | bytes 442376 | tf_op jit(solution)/shard_map/ppermute | solution.py:595
  29.7 9.0 %collective-permute-start.4 = (bf16[4,144,128]{2,1,0:T(8,128)(2,1)S(1)}, bf16[4,144,128]{2,1,0:T(8,128)(2,1)S(1)}, u32[]{:S(2)}, u32[]{:S(2)}) collective-permute-start(bf16[4,144,128]{2,1,0:T(8,128)(2,1)S(1)} %get-tuple-element.46.rest_0_), channel_id=1, source_target_pairs={{0,1},{1,0},{2,3},{3,2},{4,5},{5,4},{6,7},{7,6},{8,9},{9,8},{10,11... | collective-permute-start | bytes 442376 | tf_op jit(solution)/shard_map/ppermute | solution.py:595

commit v4 on v3

--- a/solution.py
+++ b/solution.py
@@ -8,7 +8,7 @@
 CAP = 4
 KAPPA = 0.24
 SHARPNESS = 8.0
-TAIL = 8
+TAIL = 16
 TAGS = 16
 CHUNK = 16
 UNROLL = 8
@@ -70,17 +70,29 @@
 
     row8 = sublanes((TAIL, cols))
 
+    def split(value):
+        high = value.astype(BF16).astype(F32)
+        return high, value - high
+
     def side_weight(column):
-        return jnp.where(row8 == 0, spread(column[:half]), spread(column[half:]))
+        high0, low0 = split(spread(column[:half]))
+        high1, low1 = split(spread(column[half:]))
+        lows = jnp.where(row8 == 2, low0, low1)
+        return jnp.where(row8 == 0, high0, jnp.where(row8 == 1, high1, lows))
 
     w_right = side_weight(weight[:, cols - 1:])
     w_left = side_weight(weight[:, :1])
-    cols_a[2 * members:, :] = jnp.where(f_even, w_right, w_left)
-    cols_b[2 * members:, :] = jnp.where(f_even, w_left, w_right)
-    w_top = jnp.broadcast_to(weight[:1, :], (TAIL, cols))
-    w_bottom = jnp.broadcast_to(weight[rows - 1:, :], (TAIL, cols))
-    rows_a[2 * members:, :] = jnp.where(t_even, w_bottom, w_top)
-    rows_b[2 * members:, :] = jnp.where(t_even, w_top, w_bottom)
+    cols_a[2 * members:, :] = jnp.where(f_even, w_right, w_left).astype(BF16)
+    cols_b[2 * members:, :] = jnp.where(f_even, w_left, w_right).astype(BF16)
+
+    def rim_weight(row):
+        high, low = split(row)
+        return jnp.where(row8 == 0, high, low)
+
+    w_top = rim_weight(weight[:1, :])
+    w_bottom = rim_weight(weight[rows - 1:, :])
+    rows_a[2 * members:, :] = jnp.where(t_even, w_bottom, w_top).astype(BF16)
+    rows_b[2 * members:, :] = jnp.where(t_even, w_top, w_bottom).astype(BF16)
     for c in range(tiles.shape[0]):
         value = scale_v[:, c:c + 1].astype(F32)
         tiles_out[c, depth:, :] = jnp.broadcast_to(value, (TAGS, cols)).astype(BF16)
@@ -114,12 +126,12 @@
     right = jnp.where(low, even, pltpu.roll(odd, 2, 1))
     left = jnp.where(low, pltpu.roll(even, cols - 2, 1), odd)
     own[...] = jnp.where(lanes(wide) % 2 == 0, pltpu.roll(right, cols - 1, 1), pltpu.roll(left, 1, 1))
-    cols_a[:2 * members, :] = jnp.where(f_even, right, left)
-    cols_b[:2 * members, :] = jnp.where(f_even, left, right)
+    cols_a[:2 * members, :] = jnp.where(f_even, right, left).astype(BF16)
+    cols_b[:2 * members, :] = jnp.where(f_even, left, right).astype(BF16)
     for k in range(2):
         to = pl.ds(k * members, members)
-        rows_a[to, :] = turned[jnp.where(t_even, rows - 2, 0) + k]
-        rows_b[to, :] = turned[jnp.where(t_even, 0, rows - 2) + k]
+        rows_a[to, :] = turned[jnp.where(t_even, rows - 2, 0) + k].astype(BF16)
+        rows_b[to, :] = turned[jnp.where(t_even, 0, rows - 2) + k].astype(BF16)
 
 
 def corners_kernel(place, rows_a, rows_b, got_a, got_b, out_a, out_b):
@@ -129,8 +141,9 @@
     f_even = place[1] == 0
     side = (members, cols)
     swap = (lanes(side) % 2 == 1) == f_even
-    top = jnp.where(swap, got_b[:members, :], got_a[:members, :])
-    bottom = jnp.where(swap, got_b[members:2 * members, :], got_a[members:2 * members, :])
+    top = jnp.where(swap, got_b[:members, :].astype(F32), got_a[:members, :].astype(F32))
+    low = slice(members, 2 * members)
+    bottom = jnp.where(swap, got_b[low, :].astype(F32), got_a[low, :].astype(F32))
 
     def to_row(pair, first):
         east = jnp.where(lanes(side) == 2 * sublanes(side), pair[:, first:first + 1], 0.0)
@@ -139,11 +152,12 @@
 
     top_row = to_row(top, 0)
     bottom_row = to_row(bottom, cols - 2)
-    out_a[...] = rows_a[...]
-    out_b[...] = rows_b[...]
-    at = 2 * members + 1
-    out_a[at:at + 1, :] = jnp.where(t_even, bottom_row, top_row)
-    out_b[at:at + 1, :] = jnp.where(t_even, top_row, bottom_row)
+    last = 2 * members
+    second = sublanes((TAIL, cols)) == 1
+    for out, ref, first, other in ((out_a, rows_a, bottom_row, top_row), (out_b, rows_b, top_row, bottom_row)):
+        out[:last, :] = ref[:last, :]
+        corner = jnp.where(t_even, first, other)
+        out[last:, :] = jnp.where(second, corner, ref[last:, :].astype(F32)).astype(BF16)
 
 
 def hubs_kernel(
@@ -159,15 +173,18 @@
     lane = lanes(side)
     even_lane = lane % 2 == 0
 
-    tail_n = jnp.where(t_even, rows_b[2 * members:, :], rows_a[2 * members:, :])
-    tail_s = jnp.where(t_even, rows_a[2 * members:, :], rows_b[2 * members:, :])
+    tail_a = rows_a[2 * members:, :].astype(F32)
+    tail_b = rows_b[2 * members:, :].astype(F32)
+    tail_n = jnp.where(t_even, tail_b, tail_a)
+    tail_s = jnp.where(t_even, tail_a, tail_b)
     for k in range(2):
         at = slice(k * members, (k + 1) * members)
-        strips[k] = jnp.where(t_even, rows_b[at, :], rows_a[at, :])
-        strips[2 + k] = jnp.where(t_even, rows_a[at, :], rows_b[at, :])
-    coef[0:8, :] = KAPPA * tail_n
+        row_a, row_b = rows_a[at, :].astype(F32), rows_b[at, :].astype(F32)
+        strips[k] = jnp.where(t_even, row_b, row_a)
+        strips[2 + k] = jnp.where(t_even, row_a, row_b)
+    coef[0:8, :] = jnp.broadcast_to(KAPPA * (tail_n[0:1] + tail_n[2:3]), (8, cols))
     coef[8:8 + rows, :] = KAPPA * weight[...]
-    coef[8 + rows:, :] = KAPPA * tail_s
+    coef[8 + rows:, :] = jnp.broadcast_to(KAPPA * (tail_s[0:1] + tail_s[2:3]), (8, cols))
 
     def corner(tail):
         row = jnp.broadcast_to(tail[1:2, :], side)
@@ -180,14 +197,14 @@
     halves = []
     for k in range(2):
         at = slice(k * members, (k + 1) * members)
-        a, b = cols_a[at, :], cols_b[at, :]
+        a, b = cols_a[at, :].astype(F32), cols_b[at, :].astype(F32)
         from_e = jnp.where(f_even, a, b)
         from_w = jnp.where(f_even, b, a)
         close = jnp.where(even_lane, from_e, from_w)
         far = jnp.where(even_lane, pltpu.roll(from_e, cols - 1, 1), pltpu.roll(from_w, 1, 1))
         near[at, :] = close
         halves.append((close, far))
-    wa, wb = cols_a[2 * members:, :], cols_b[2 * members:, :]
+    wa, wb = cols_a[2 * members:, :].astype(F32), cols_b[2 * members:, :].astype(F32)
     w_e = jnp.where(f_even, wa, wb)
     w_w = jnp.where(f_even, wb, wa)
     w_packed = jnp.where(lanes((TAIL, cols)) % 2 == 0, w_e, w_w)
@@ -202,7 +219,8 @@
         at = slice(k * members, (k + 1) * members)
         close, far = halves[k]
         around = (n + s) + (far + own[at, :])
-        halo1[at, :] = close + KAPPA * w_packed[k:k + 1, :] * (around - 4.0 * close)
+        w = KAPPA * (w_packed[k:k + 1, :] + w_packed[k + 2:k + 3, :])
+        halo1[at, :] = close + w * (around - 4.0 * close)
     beside[0:members, :] = jnp.where(lane == 0, west_n, east_n)
     beside[members:2 * members, :] = pltpu.roll(near1, cols - 1, 1)
     beside[2 * members:3 * members, :] = pltpu.roll(near0, 1, 1)
@@ -413,8 +431,8 @@
 
 
 def land_kernel(place, landed, kept, grow, *rest):
-    blocks, rest = rest[:-12], rest[-12:]
-    out, table, base, gate, carried, tags_v, tags_s, owner, lead, tag_sem, row_sem, out_sem = rest
+    blocks, rest = rest[:-13], rest[-13:]
+    out, table, base, gate, carried, tags_v, tags_s, owner, lead, final, tag_sem, row_sem, out_sem = rest
     per = blocks[0].shape[0]
     bands, cols = tags_v.shape
     stride = landed.shape[0] // bands
@@ -451,7 +469,9 @@
         at = jnp.maximum(row, 0)
         mine = owner[at]
         fresh = jnp.logical_and(row >= 0, mine < 0)
-        lead[s] = jnp.where(row < 0, slots, jnp.where(mine < 0, s, mine))
+        leader = jnp.where(row < 0, slots, jnp.where(mine < 0, s, mine))
+        lead[s] = leader
+        final[leader] = s
 
         @pl.when(fresh)
         def _():
@@ -462,6 +482,7 @@
         return count + jnp.where(fresh, 1, 0)
 
     count = lax.fori_loop(0, slots, claim, 0)
+    final[slots] = -1
 
     def product(t, carry):
         for n in range(CAP):
@@ -485,21 +506,21 @@
         for n in range(CAP):
             to = lead[t * CAP + n]
             base[to] = base[to] + carried[t * CAP + n] * gate[to]
+        for n in range(CAP):
+            to = lead[t * CAP + n]
+
+            @pl.when(final[to] == t * CAP + n)
+            def _():
+                store(tags_s[t, n], to).start()
+
         return carry
 
     lax.fori_loop(0, bands, add, 0)
-
-    def send(s, carry):
-        @pl.when(lead[s] == s)
-        def _():
-            store(tags_s[s // CAP, s % CAP], s).start()
-        return carry
 
     def finish(s, carry):
         store(0, 0).wait()
         return carry
 
-    lax.fori_loop(0, slots, send, 0)
     lax.fori_loop(0, count, finish, 0)
 
 
@@ -556,7 +577,7 @@
     hubs, share = hub_row.reshape(-1), jump_share.reshape(-1)
     sds = jax.ShapeDtypeStruct
     per, depth = flow_tiles.shape[:2]
-    message = sds((2 * members + TAIL, cols), F32)
+    message = sds((2 * members + TAIL, cols), BF16)
     pack = sds((2 * members, cols), F32)
     cols_a, cols_b, rows_a, rows_b, own, weight, tiles, turned = pl.pallas_call(
         edges_kernel,
@@ -663,6 +684,7 @@
             pltpu.SMEM((bands, cols), jnp.int32),
             pltpu.SMEM((rows,), jnp.int32),
             pltpu.SMEM((slots,), jnp.int32),
+            pltpu.SMEM((slots + 1,), jnp.int32),
             pltpu.SemaphoreType.DMA,
             pltpu.SemaphoreType.DMA,
             pltpu.SemaphoreType.DMA,

time: 44.8 us -> 43.9 us (0.980)
  transfers between devices with their start and end apart: 8 -> 8, of which waited for: 2 -> 2; matrix products, arithmetic and copies ran while one was open for 0% -> 0% of each run, Pallas kernels for 26% -> 27%
where the time goes in v4:
time: 43.9 us; the launch traced here: 43.6 us
  Pallas kernels  23.1 us (53%)
  starting transfers between devices  16.5 us (38%)
  waiting for transfers between devices  3.69 us (8%)
    pallas_call x1, Pallas kernels, local(): pl.pallas_call(bulk_kernel, out_shape=sds(density.shape, F32), in_specs=[...  8.47 us
    all_to_all x1, starting transfers between devices, local(): lax.all_to_all(sent, 'tile', split_axis=0, concat_axis=0, tiled=True)  7.03 us
    ppermute x1, starting transfers between devices, local(): got_b = lax.ppermute(cols_b, 'flow', far_pairs(flows))  4.47 us
    pallas_call x1, Pallas kernels, local(): pl.pallas_call(land_kernel, out_shape=sds(density.shape, F32), in_specs=[...  3.91 us
    pallas_call x1, Pallas kernels, local(): pl.pallas_call(edges_kernel, out_shape=(message, message, message, messag...  3.76 us
    pallas_call x1, Pallas kernels, local(): pl.pallas_call(hubs_kernel, out_shape=(sds((bands * stride, cols), BF16),...  3.15 us
    pallas_call x1, Pallas kernels, local(): pl.pallas_call(grow_kernel, out_shape=pltpu.HBM(density.shape, F32), in_s...  3.13 us
    ppermute x3, starting transfers between devices, swap(): return lax.ppermute(x, 'flow', [(i, i ^ bit) for i in range(flows)])  2.39 us
  transfers between devices with their start and end apart: 8, of which 2 were waited for; matrix products, arithmetic and copies ran while one was open for 0% of the time, Pallas kernels for 27%

profile of v4, /device:TPU:1, one launch (start us, length us, event | category | flops | bytes accessed | tf_op | source)
XLA Modules:
  0.0 43.6 jit_solution(10551382034465525991)
XLA Ops:
  0.0 0.1 pad_add_fusion.place
  0.1 3.8 %edges.1 = (bf16[144,128]{1,0:T(8,128)(2,1)S(1)}, bf16[144,128]{1,0:T(8,128)(2,1)S(1)}, bf16[144,128]{1,0:T(8,128)(2,1)S(1)}, bf16[144,128]{1,0:T(8,128)(2,1)S(1...) custom-call(s32[4]{0:T(128)S(1)} %pad_add_fusion.place, ...), custom_call_target="tpu_custom_call" | custom-call | tf_op jit(solution)/shard_map/edges/pallas_call | solution.py:582
  3.8 0.0 copy-start
  3.9 0.0 copy-start.1
  3.9 0.0 copy-start.2
  3.9 0.0 copy-start.3
  3.9 0.0 copy-start.4
  3.9 0.1 collective-permute-start
  4.0 4.5 %collective-permute-start.1 = (bf16[144,128]{1,0:T(8,128)(2,1)S(1)}, bf16[144,128]{1,0:T(8,128)(2,1)S(1)}, u32[]{:S(2)}, u32[]{:S(2)}) collective-permute-start(bf16[144,128]{1,0:T(8,128)(2,1)S(1)} %get-tuple-element.30), channel_id=1, source_target_pairs={{1,2},{2,1},{5,6},{6,5},{9,10},{10,9},{13,14},{14,13},{17,18},{18,... | collective-permute-start | bytes 110600 | tf_op jit(solution)/shard_map/ppermute | solution.py:602
  8.5 0.0 collective-permute-done.got_a.cols_a
  8.5 1.9 %collective-permute-done.1.got_b.cols_b = bf16[144,128]{1,0:T(8,128)(2,1)S(1)} collective-permute-done((bf16[144,128]{1,0:T(8,128)(2,1)S(1)}, bf16[144,128]{1,0:T(8,128)(2,1)S(1)}, u32[]{:S(2)}, u32[]{:S(2)}) %collective-permute-start.1) | collective-permute-done | bytes 36896 | tf_op jit(solution)/shard_map/ppermute | solution.py:602
  10.4 0.6 %corners.1 = (bf16[144,128]{1,0:T(8,128)(2,1)S(1)}, bf16[144,128]{1,0:T(8,128)(2,1)S(1)}) custom-call(s32[4]{0:T(128)S(1)} %pad_add_fusion.place, bf16[144,128]{1,0:T(8,128)(2,1)S(1)} %get-tuple-element.27.rows_a, bf16[144,128]{1,0:T(8,128)(2,1)S(1)} %get-tuple-element.28.rows_b, bf16[144,128]{1,0:T(8,128)(2,1)S(1)} %collective-permute-done.got_a.cols_a, ...), custom_call_target="tpu_custom_call" | custom-call | tf_op jit(solution)/shard_map/corners/pallas_call | solution.py:603
  11.1 1.9 %collective-permute-start.2 = (bf16[144,128]{1,0:T(8,128)(2,1)S(1)}, bf16[144,128]{1,0:T(8,128)(2,1)S(1)}, u32[]{:S(2)}, u32[]{:S(2)}) collective-permute-start(bf16[144,128]{1,0:T(8,128)(2,1)S(1)} %get-tuple-element.37), channel_id=1, source_target_pairs={{0,4},{4,0},{8,12},{12,8},{16,20},{20,16},{24,28},{28,24},{1,5},{5... | collective-permute-start | bytes 110600 | tf_op jit(solution)/shard_map/ppermute | solution.py:612
  12.9 0.7 %collective-permute-start.3 = (bf16[144,128]{1,0:T(8,128)(2,1)S(1)}, bf16[144,128]{1,0:T(8,128)(2,1)S(1)}, u32[]{:S(2)}, u32[]{:S(2)}) collective-permute-start(bf16[144,128]{1,0:T(8,128)(2,1)S(1)} %get-tuple-element.38), channel_id=1, source_target_pairs={{4,8},{8,4},{12,16},{16,12},{20,24},{24,20},{5,9},{9,5},{13,17},{1... | collective-permute-start | bytes 110600 | tf_op jit(solution)/shard_map/ppermute | solution.py:613
  13.6 3.1 %grow.1 = f32[64,128,128]{2,1,0:T(8,128)} custom-call(bf16[64,128,128]{2,1,0:T(8,128)(2,1)} %draw, f32[128,128]{1,0:T(8,128)} %threshold.1), custom_call_target="tpu_custom_call" | custom-call | tf_op jit(solution)/shard_map/grow/pallas_call | solution.py:618
  16.7 0.0 collective-permute-done.3.rows_b
  16.8 3.1 %hubs.1 = (bf16[2176,128]{1,0:T(8,128)(2,1)}, f32[128,128]{1,0:T(8,128)S(1)}, f32[128,128]{1,0:T(8,128)S(1)}, f32[256,128]{1,0:T(8,128)S(1)}, f32[144,128]{1,0:T(8,128)S(1)}, /*index=5*/f32[4,64,128]{2,1,0:T(8,128)S(1)}) custom-call(s32[4]{0:T(128)S(1)} %pad_add_fusion.place, s32[16]{0:T(128)S(1)} %bitcast.13, s32[16]{0:T(128)S(1)} %bitcast.17, ...), custom_call_target="tpu_custom_call" | custom-call | tf_op jit(solution)/shard_map/hubs/pallas_call | solution.py:640
  19.9 7.0 %all-to-all-start = ((bf16[8,272,128]{2,1,0:T(8,128)(2,1)}), bf16[8,272,128]{2,1,0:T(8,128)(2,1)S(1)}, u32[]{:S(2)}, u32[]{:S(2)}) async-start(bf16[8,272,128]{2,1,0:T(8,128)(2,1)} %bitcast.10), calls=%async_computation | async-start | bytes 1114112 | tf_op jit(solution)/shard_map/all_to_all | solution.py:652
  27.0 1.9 %collective-permute-start.6 = (bf16[4,144,128]{2,1,0:T(8,128)(2,1)S(1)}, bf16[4,144,128]{2,1,0:T(8,128)(2,1)S(1)}, u32[]{:S(2)}, u32[]{:S(2)}) collective-permute-start(bf16[4,144,128]{2,1,0:T(8,128)(2,1)S(1)} %get-tuple-element.46.rest_0_), channel_id=1, source_target_pairs={{0,3},{1,2},{2,1},{3,0},{4,7},{5,6},{6,5},{7,4},{8,11},{9,10},{10,... | collective-permute-start | bytes 442376 | tf_op jit(solution)/shard_map/ppermute | solution.py:616
  28.9 0.0 collective-permute-start.5
  28.9 0.5 %collective-permute-start.4 = (bf16[4,144,128]{2,1,0:T(8,128)(2,1)S(1)}, bf16[4,144,128]{2,1,0:T(8,128)(2,1)S(1)}, u32[]{:S(2)}, u32[]{:S(2)}) collective-permute-start(bf16[4,144,128]{2,1,0:T(8,128)(2,1)S(1)} %get-tuple-element.46.rest_0_), channel_id=1, source_target_pairs={{0,1},{1,0},{2,3},{3,2},{4,5},{5,4},{6,7},{7,6},{8,9},{9,8},{10,11... | collective-permute-start | bytes 442376 | tf_op jit(solution)/shard_map/ppermute | solution.py:616
  29.4 8.5 %bulk.1.kept = f32[64,128,128]{2,1,0:T(8,128)} custom-call(s32[16]{0:T(128)S(1)} %bitcast.14, f32[16]{0:T(128)S(1)} %bitcast.16, f32[64,128,128]{2,1,0:T(8,128)} %density.3, f32[64,128,128]{2,1,0:T(8,128)} %grow.1, f32[144,128]{1,0:T(8,128)S(1)} %get-tuple-element.41.coef, f32[4,64,128]{2,1,0:T(8,128)S(1)} %get-tuple-element.42.strips, ...), custom_call_target="tpu_custom_call" | custom-call | tf_op jit(solution)/shard_map/bulk/pallas_call | solution.py:653
  37.9 1.8 %all-to-all-done = bf16[8,272,128]{2,1,0:T(8,128)(2,1)S(1)} async-done(((bf16[8,272,128]{2,1,0:T(8,128)(2,1)}), bf16[8,272,128]{2,1,0:T(8,128)(2,1)S(1)}, u32[]{:S(2)}, u32[]{:S(2)}) %all-to-all-start) | async-done | bytes 557088 | tf_op jit(solution)/shard_map/all_to_all | solution.py:652
  39.6 3.9 %land.1 = f32[64,128,128]{2,1,0:T(8,128)} custom-call(s32[4]{0:T(128)S(1)} %pad_add_fusion.place, bf16[2176,128]{1,0:T(8,128)(2,1)S(1)} %bitcast.12, f32[64,128,128]{2,1,0:T(8,128)} %bulk.1.kept, f32[64,128,128]{2,1,0:T(8,128)} %grow.1, bf16[4,144,128]{2,1,0:T(8,128)(2,1)S(1)} %get-tuple-element.46.rest_0_, ...), custom_call_target="tpu_custom_call", output_to_operand_aliasing={{}: (2, {})} | custom-call | tf_op jit(solution)/shard_map/land/pallas_call | solution.py:672
  (9 shorter events, 0.0 us)
Async XLA Ops:
  3.8 12.9 %copy-start = (s32[1,16]{1,0:T(1,128)S(1)}, s32[1,16]{1,0:T(1,128)}, u32[]{:S(2)}) copy-start(s32[1,16]{1,0:T(1,128)} %param.17) | copy-start | bytes 196
  3.9 12.9 %copy-start.1 = (f32[1,16]{1,0:T(1,128)S(1)}, f32[1,16]{1,0:T(1,128)}, u32[]{:S(2)}) copy-start(f32[1,16]{1,0:T(1,128)} %param.21) | copy-start | bytes 196
  3.9 12.9 %copy-start.2 = (s32[1,16,1]{1,2,0:T(1,128)S(1)}, s32[1,16,1]{1,2,0:T(1,128)}, u32[]{:S(2)}) copy-start(s32[1,16,1]{1,2,0:T(1,128)} %param.18) | copy-start | bytes 196
  3.9 12.9 %copy-start.3 = (s32[1,16]{1,0:T(1,128)S(1)}, s32[1,16]{1,0:T(1,128)}, u32[]{:S(2)}) copy-start(s32[1,16]{1,0:T(1,128)} %param.19) | copy-start | bytes 196
  3.9 12.9 %copy-start.4 = (s32[1,16]{1,0:T(1,128)S(1)}, s32[1,16]{1,0:T(1,128)}, u32[]{:S(2)}) copy-start(s32[1,16]{1,0:T(1,128)} %param.20) | copy-start | bytes 196
  3.9 4.6 %collective-permute-start = (bf16[144,128]{1,0:T(8,128)(2,1)S(1)}, bf16[144,128]{1,0:T(8,128)(2,1)S(1)}, u32[]{:S(2)}, u32[]{:S(2)}) collective-permute-start(bf16[144,128]{1,0:T(8,128)(2,1)S(1)} %get-tuple-element.29), channel_id=1, source_target_pairs={{0,1},{1,0},{2,3},{3,2},{4,5},{5,4},{6,7},{7,6},{8,9},{9,8},{10,11... | collective-permute-start | bytes 110600 | tf_op jit(solution)/shard_map/ppermute | solution.py:601
  4.0 6.4 %collective-permute-start.1 = (bf16[144,128]{1,0:T(8,128)(2,1)S(1)}, bf16[144,128]{1,0:T(8,128)(2,1)S(1)}, u32[]{:S(2)}, u32[]{:S(2)}) collective-permute-start(bf16[144,128]{1,0:T(8,128)(2,1)S(1)} %get-tuple-element.30), channel_id=1, source_target_pairs={{1,2},{2,1},{5,6},{6,5},{9,10},{10,9},{13,14},{14,13},{17,18},{18,... | collective-permute-start | bytes 110600 | tf_op jit(solution)/shard_map/ppermute | solution.py:602
  11.1 5.7 %collective-permute-start.2 = (bf16[144,128]{1,0:T(8,128)(2,1)S(1)}, bf16[144,128]{1,0:T(8,128)(2,1)S(1)}, u32[]{:S(2)}, u32[]{:S(2)}) collective-permute-start(bf16[144,128]{1,0:T(8,128)(2,1)S(1)} %get-tuple-element.37), channel_id=1, source_target_pairs={{0,4},{4,0},{8,12},{12,8},{16,20},{20,16},{24,28},{28,24},{1,5},{5... | collective-permute-start | bytes 110600 | tf_op jit(solution)/shard_map/ppermute | solution.py:612
  12.9 3.8 %collective-permute-start.3 = (bf16[144,128]{1,0:T(8,128)(2,1)S(1)}, bf16[144,128]{1,0:T(8,128)(2,1)S(1)}, u32[]{:S(2)}, u32[]{:S(2)}) collective-permute-start(bf16[144,128]{1,0:T(8,128)(2,1)S(1)} %get-tuple-element.38), channel_id=1, source_target_pairs={{4,8},{8,4},{12,16},{16,12},{20,24},{24,20},{5,9},{9,5},{13,17},{1... | collective-permute-start | bytes 110600 | tf_op jit(solution)/shard_map/ppermute | solution.py:613
  19.9 19.7 %all-to-all-start = ((bf16[8,272,128]{2,1,0:T(8,128)(2,1)}), bf16[8,272,128]{2,1,0:T(8,128)(2,1)S(1)}, u32[]{:S(2)}, u32[]{:S(2)}) async-start(bf16[8,272,128]{2,1,0:T(8,128)(2,1)} %bitcast.10), calls=%async_computation | async-start | bytes 1114112 | tf_op jit(solution)/shard_map/all_to_all | solution.py:652
  27.0 10.9 %collective-permute-start.6 = (bf16[4,144,128]{2,1,0:T(8,128)(2,1)S(1)}, bf16[4,144,128]{2,1,0:T(8,128)(2,1)S(1)}, u32[]{:S(2)}, u32[]{:S(2)}) collective-permute-start(bf16[4,144,128]{2,1,0:T(8,128)(2,1)S(1)} %get-tuple-element.46.rest_0_), channel_id=1, source_target_pairs={{0,3},{1,2},{2,1},{3,0},{4,7},{5,6},{6,5},{7,4},{8,11},{9,10},{10,... | collective-permute-start | bytes 442376 | tf_op jit(solution)/shard_map/ppermute | solution.py:616
  28.9 9.0 %collective-permute-start.5 = (bf16[4,144,128]{2,1,0:T(8,128)(2,1)S(1)}, bf16[4,144,128]{2,1,0:T(8,128)(2,1)S(1)}, u32[]{:S(2)}, u32[]{:S(2)}) collective-permute-start(bf16[4,144,128]{2,1,0:T(8,128)(2,1)S(1)} %get-tuple-element.46.rest_0_), channel_id=1, source_target_pairs={{0,2},{1,3},{2,0},{3,1},{4,6},{5,7},{6,4},{7,5},{8,10},{9,11},{10,... | collective-permute-start | bytes 442376 | tf_op jit(solution)/shard_map/ppermute | solution.py:616
  28.9 9.0 %collective-permute-start.4 = (bf16[4,144,128]{2,1,0:T(8,128)(2,1)S(1)}, bf16[4,144,128]{2,1,0:T(8,128)(2,1)S(1)}, u32[]{:S(2)}, u32[]{:S(2)}) collective-permute-start(bf16[4,144,128]{2,1,0:T(8,128)(2,1)S(1)} %get-tuple-element.46.rest_0_), channel_id=1, source_target_pairs={{0,1},{1,0},{2,3},{3,2},{4,5},{5,4},{6,7},{7,6},{8,9},{9,8},{10,11... | collective-permute-start | bytes 442376 | tf_op jit(solution)/shard_map/ppermute | solution.py:616

commit v5 on v4

--- a/solution.py
+++ b/solution.py
@@ -11,7 +11,7 @@
 TAIL = 16
 TAGS = 16
 CHUNK = 16
-UNROLL = 8
+UNROLL = 16
 STEP = 16
 GROW = 16
 MIB = 1024 * 1024

time: 43.9 us -> 43.6 us (level)
  no operation moved by 1% of the time
where the time goes in v5:
time: 43.6 us; the launch traced here: 43.3 us
  Pallas kernels  22.7 us (52%)
  starting transfers between devices  16.5 us (38%)
  waiting for transfers between devices  3.71 us (9%)
    pallas_call x1, Pallas kernels, local(): pl.pallas_call(bulk_kernel, out_shape=sds(density.shape, F32), in_specs=[...  8.45 us
    all_to_all x1, starting transfers between devices, local(): lax.all_to_all(sent, 'tile', split_axis=0, concat_axis=0, tiled=True)  7.03 us
    ppermute x1, starting transfers between devices, local(): got_b = lax.ppermute(cols_b, 'flow', far_pairs(flows))  4.47 us
    pallas_call x1, Pallas kernels, local(): pl.pallas_call(land_kernel, out_shape=sds(density.shape, F32), in_specs=[...  3.84 us
    pallas_call x1, Pallas kernels, local(): pl.pallas_call(edges_kernel, out_shape=(message, message, message, messag...  3.76 us
    pallas_call x1, Pallas kernels, local(): pl.pallas_call(grow_kernel, out_shape=pltpu.HBM(density.shape, F32), in_s...  3.13 us
    pallas_call x1, Pallas kernels, local(): pl.pallas_call(hubs_kernel, out_shape=(sds((bands * stride, cols), BF16),...  2.92 us
    ppermute x3, starting transfers between devices, swap(): return lax.ppermute(x, 'flow', [(i, i ^ bit) for i in range(flows)])  2.39 us
  transfers between devices with their start and end apart: 8, of which 2 were waited for; matrix products, arithmetic and copies ran while one was open for 0% of the time, Pallas kernels for 27%

profile of v5, /device:TPU:1, one launch (start us, length us, event | category | flops | bytes accessed | tf_op | source)
XLA Modules:
  0.0 43.3 jit_solution(1306037815398838878)
XLA Ops:
  0.0 0.1 pad_add_fusion.place
  0.1 3.8 %edges.1 = (bf16[144,128]{1,0:T(8,128)(2,1)S(1)}, bf16[144,128]{1,0:T(8,128)(2,1)S(1)}, bf16[144,128]{1,0:T(8,128)(2,1)S(1)}, bf16[144,128]{1,0:T(8,128)(2,1)S(1...) custom-call(s32[4]{0:T(128)S(1)} %pad_add_fusion.place, ...), custom_call_target="tpu_custom_call" | custom-call | tf_op jit(solution)/shard_map/edges/pallas_call | solution.py:582
  3.8 0.0 copy-start
  3.9 0.0 copy-start.1
  3.9 0.0 copy-start.2
  3.9 0.0 copy-start.3
  3.9 0.0 copy-start.4
  3.9 0.1 collective-permute-start
  4.0 4.5 %collective-permute-start.1 = (bf16[144,128]{1,0:T(8,128)(2,1)S(1)}, bf16[144,128]{1,0:T(8,128)(2,1)S(1)}, u32[]{:S(2)}, u32[]{:S(2)}) collective-permute-start(bf16[144,128]{1,0:T(8,128)(2,1)S(1)} %get-tuple-element.30), channel_id=1, source_target_pairs={{1,2},{2,1},{5,6},{6,5},{9,10},{10,9},{13,14},{14,13},{17,18},{18,... | collective-permute-start | bytes 110600 | tf_op jit(solution)/shard_map/ppermute | solution.py:602
  8.5 0.0 collective-permute-done.got_a.cols_a
  8.5 1.9 %collective-permute-done.1.got_b.cols_b = bf16[144,128]{1,0:T(8,128)(2,1)S(1)} collective-permute-done((bf16[144,128]{1,0:T(8,128)(2,1)S(1)}, bf16[144,128]{1,0:T(8,128)(2,1)S(1)}, u32[]{:S(2)}, u32[]{:S(2)}) %collective-permute-start.1) | collective-permute-done | bytes 36896 | tf_op jit(solution)/shard_map/ppermute | solution.py:602
  10.4 0.6 %corners.1 = (bf16[144,128]{1,0:T(8,128)(2,1)S(1)}, bf16[144,128]{1,0:T(8,128)(2,1)S(1)}) custom-call(s32[4]{0:T(128)S(1)} %pad_add_fusion.place, bf16[144,128]{1,0:T(8,128)(2,1)S(1)} %get-tuple-element.27.rows_a, bf16[144,128]{1,0:T(8,128)(2,1)S(1)} %get-tuple-element.28.rows_b, bf16[144,128]{1,0:T(8,128)(2,1)S(1)} %collective-permute-done.got_a.cols_a, ...), custom_call_target="tpu_custom_call" | custom-call | tf_op jit(solution)/shard_map/corners/pallas_call | solution.py:603
  11.1 1.9 %collective-permute-start.2 = (bf16[144,128]{1,0:T(8,128)(2,1)S(1)}, bf16[144,128]{1,0:T(8,128)(2,1)S(1)}, u32[]{:S(2)}, u32[]{:S(2)}) collective-permute-start(bf16[144,128]{1,0:T(8,128)(2,1)S(1)} %get-tuple-element.37), channel_id=1, source_target_pairs={{0,4},{4,0},{8,12},{12,8},{16,20},{20,16},{24,28},{28,24},{1,5},{5... | collective-permute-start | bytes 110600 | tf_op jit(solution)/shard_map/ppermute | solution.py:612
  12.9 0.7 %collective-permute-start.3 = (bf16[144,128]{1,0:T(8,128)(2,1)S(1)}, bf16[144,128]{1,0:T(8,128)(2,1)S(1)}, u32[]{:S(2)}, u32[]{:S(2)}) collective-permute-start(bf16[144,128]{1,0:T(8,128)(2,1)S(1)} %get-tuple-element.38), channel_id=1, source_target_pairs={{4,8},{8,4},{12,16},{16,12},{20,24},{24,20},{5,9},{9,5},{13,17},{1... | collective-permute-start | bytes 110600 | tf_op jit(solution)/shard_map/ppermute | solution.py:613
  13.6 3.1 %grow.1 = f32[64,128,128]{2,1,0:T(8,128)} custom-call(bf16[64,128,128]{2,1,0:T(8,128)(2,1)} %draw, f32[128,128]{1,0:T(8,128)} %threshold.1), custom_call_target="tpu_custom_call" | custom-call | tf_op jit(solution)/shard_map/grow/pallas_call | solution.py:618
  16.7 0.0 collective-permute-done.3.rows_b
  16.8 2.9 %hubs.1 = (bf16[2176,128]{1,0:T(8,128)(2,1)}, f32[128,128]{1,0:T(8,128)S(1)}, f32[128,128]{1,0:T(8,128)S(1)}, f32[256,128]{1,0:T(8,128)S(1)}, f32[144,128]{1,0:T(8,128)S(1)}, /*index=5*/f32[4,64,128]{2,1,0:T(8,128)S(1)}) custom-call(s32[4]{0:T(128)S(1)} %pad_add_fusion.place, s32[16]{0:T(128)S(1)} %bitcast.13, s32[16]{0:T(128)S(1)} %bitcast.17, ...), custom_call_target="tpu_custom_call" | custom-call | tf_op jit(solution)/shard_map/hubs/pallas_call | solution.py:640
  19.7 7.0 %all-to-all-start = ((bf16[8,272,128]{2,1,0:T(8,128)(2,1)}), bf16[8,272,128]{2,1,0:T(8,128)(2,1)S(1)}, u32[]{:S(2)}, u32[]{:S(2)}) async-start(bf16[8,272,128]{2,1,0:T(8,128)(2,1)} %bitcast.10), calls=%async_computation | async-start | bytes 1114112 | tf_op jit(solution)/shard_map/all_to_all | solution.py:652
  26.8 1.9 %collective-permute-start.6 = (bf16[4,144,128]{2,1,0:T(8,128)(2,1)S(1)}, bf16[4,144,128]{2,1,0:T(8,128)(2,1)S(1)}, u32[]{:S(2)}, u32[]{:S(2)}) collective-permute-start(bf16[4,144,128]{2,1,0:T(8,128)(2,1)S(1)} %get-tuple-element.46.rest_0_), channel_id=1, source_target_pairs={{0,3},{1,2},{2,1},{3,0},{4,7},{5,6},{6,5},{7,4},{8,11},{9,10},{10,... | collective-permute-start | bytes 442376 | tf_op jit(solution)/shard_map/ppermute | solution.py:616
  28.7 0.0 collective-permute-start.5
  28.7 0.5 %collective-permute-start.4 = (bf16[4,144,128]{2,1,0:T(8,128)(2,1)S(1)}, bf16[4,144,128]{2,1,0:T(8,128)(2,1)S(1)}, u32[]{:S(2)}, u32[]{:S(2)}) collective-permute-start(bf16[4,144,128]{2,1,0:T(8,128)(2,1)S(1)} %get-tuple-element.46.rest_0_), channel_id=1, source_target_pairs={{0,1},{1,0},{2,3},{3,2},{4,5},{5,4},{6,7},{7,6},{8,9},{9,8},{10,11... | collective-permute-start | bytes 442376 | tf_op jit(solution)/shard_map/ppermute | solution.py:616
  29.1 8.5 %bulk.1.kept = f32[64,128,128]{2,1,0:T(8,128)} custom-call(s32[16]{0:T(128)S(1)} %bitcast.14, f32[16]{0:T(128)S(1)} %bitcast.16, f32[64,128,128]{2,1,0:T(8,128)} %density.3, f32[64,128,128]{2,1,0:T(8,128)} %grow.1, f32[144,128]{1,0:T(8,128)S(1)} %get-tuple-element.41.coef, f32[4,64,128]{2,1,0:T(8,128)S(1)} %get-tuple-element.42.strips, ...), custom_call_target="tpu_custom_call" | custom-call | tf_op jit(solution)/shard_map/bulk/pallas_call | solution.py:653
  37.6 1.8 %all-to-all-done = bf16[8,272,128]{2,1,0:T(8,128)(2,1)S(1)} async-done(((bf16[8,272,128]{2,1,0:T(8,128)(2,1)}), bf16[8,272,128]{2,1,0:T(8,128)(2,1)S(1)}, u32[]{:S(2)}, u32[]{:S(2)}) %all-to-all-start) | async-done | bytes 557088 | tf_op jit(solution)/shard_map/all_to_all | solution.py:652
  39.4 3.8 %land.1 = f32[64,128,128]{2,1,0:T(8,128)} custom-call(s32[4]{0:T(128)S(1)} %pad_add_fusion.place, bf16[2176,128]{1,0:T(8,128)(2,1)S(1)} %bitcast.12, f32[64,128,128]{2,1,0:T(8,128)} %bulk.1.kept, f32[64,128,128]{2,1,0:T(8,128)} %grow.1, bf16[4,144,128]{2,1,0:T(8,128)(2,1)S(1)} %get-tuple-element.46.rest_0_, ...), custom_call_target="tpu_custom_call", output_to_operand_aliasing={{}: (2, {})} | custom-call | tf_op jit(solution)/shard_map/land/pallas_call | solution.py:672
  (9 shorter events, 0.0 us)
Async XLA Ops:
  3.8 12.9 %copy-start = (s32[1,16]{1,0:T(1,128)S(1)}, s32[1,16]{1,0:T(1,128)}, u32[]{:S(2)}) copy-start(s32[1,16]{1,0:T(1,128)} %param.17) | copy-start | bytes 196
  3.9 12.9 %copy-start.1 = (f32[1,16]{1,0:T(1,128)S(1)}, f32[1,16]{1,0:T(1,128)}, u32[]{:S(2)}) copy-start(f32[1,16]{1,0:T(1,128)} %param.21) | copy-start | bytes 196
  3.9 12.9 %copy-start.2 = (s32[1,16,1]{1,2,0:T(1,128)S(1)}, s32[1,16,1]{1,2,0:T(1,128)}, u32[]{:S(2)}) copy-start(s32[1,16,1]{1,2,0:T(1,128)} %param.18) | copy-start | bytes 196
  3.9 12.9 %copy-start.3 = (s32[1,16]{1,0:T(1,128)S(1)}, s32[1,16]{1,0:T(1,128)}, u32[]{:S(2)}) copy-start(s32[1,16]{1,0:T(1,128)} %param.19) | copy-start | bytes 196
  3.9 12.9 %copy-start.4 = (s32[1,16]{1,0:T(1,128)S(1)}, s32[1,16]{1,0:T(1,128)}, u32[]{:S(2)}) copy-start(s32[1,16]{1,0:T(1,128)} %param.20) | copy-start | bytes 196
  3.9 4.6 %collective-permute-start = (bf16[144,128]{1,0:T(8,128)(2,1)S(1)}, bf16[144,128]{1,0:T(8,128)(2,1)S(1)}, u32[]{:S(2)}, u32[]{:S(2)}) collective-permute-start(bf16[144,128]{1,0:T(8,128)(2,1)S(1)} %get-tuple-element.29), channel_id=1, source_target_pairs={{0,1},{1,0},{2,3},{3,2},{4,5},{5,4},{6,7},{7,6},{8,9},{9,8},{10,11... | collective-permute-start | bytes 110600 | tf_op jit(solution)/shard_map/ppermute | solution.py:601
  4.0 6.4 %collective-permute-start.1 = (bf16[144,128]{1,0:T(8,128)(2,1)S(1)}, bf16[144,128]{1,0:T(8,128)(2,1)S(1)}, u32[]{:S(2)}, u32[]{:S(2)}) collective-permute-start(bf16[144,128]{1,0:T(8,128)(2,1)S(1)} %get-tuple-element.30), channel_id=1, source_target_pairs={{1,2},{2,1},{5,6},{6,5},{9,10},{10,9},{13,14},{14,13},{17,18},{18,... | collective-permute-start | bytes 110600 | tf_op jit(solution)/shard_map/ppermute | solution.py:602
  11.1 5.7 %collective-permute-start.2 = (bf16[144,128]{1,0:T(8,128)(2,1)S(1)}, bf16[144,128]{1,0:T(8,128)(2,1)S(1)}, u32[]{:S(2)}, u32[]{:S(2)}) collective-permute-start(bf16[144,128]{1,0:T(8,128)(2,1)S(1)} %get-tuple-element.37), channel_id=1, source_target_pairs={{0,4},{4,0},{8,12},{12,8},{16,20},{20,16},{24,28},{28,24},{1,5},{5... | collective-permute-start | bytes 110600 | tf_op jit(solution)/shard_map/ppermute | solution.py:612
  12.9 3.8 %collective-permute-start.3 = (bf16[144,128]{1,0:T(8,128)(2,1)S(1)}, bf16[144,128]{1,0:T(8,128)(2,1)S(1)}, u32[]{:S(2)}, u32[]{:S(2)}) collective-permute-start(bf16[144,128]{1,0:T(8,128)(2,1)S(1)} %get-tuple-element.38), channel_id=1, source_target_pairs={{4,8},{8,4},{12,16},{16,12},{20,24},{24,20},{5,9},{9,5},{13,17},{1... | collective-permute-start | bytes 110600 | tf_op jit(solution)/shard_map/ppermute | solution.py:613
  19.7 19.7 %all-to-all-start = ((bf16[8,272,128]{2,1,0:T(8,128)(2,1)}), bf16[8,272,128]{2,1,0:T(8,128)(2,1)S(1)}, u32[]{:S(2)}, u32[]{:S(2)}) async-start(bf16[8,272,128]{2,1,0:T(8,128)(2,1)} %bitcast.10), calls=%async_computation | async-start | bytes 1114112 | tf_op jit(solution)/shard_map/all_to_all | solution.py:652
  26.8 10.9 %collective-permute-start.6 = (bf16[4,144,128]{2,1,0:T(8,128)(2,1)S(1)}, bf16[4,144,128]{2,1,0:T(8,128)(2,1)S(1)}, u32[]{:S(2)}, u32[]{:S(2)}) collective-permute-start(bf16[4,144,128]{2,1,0:T(8,128)(2,1)S(1)} %get-tuple-element.46.rest_0_), channel_id=1, source_target_pairs={{0,3},{1,2},{2,1},{3,0},{4,7},{5,6},{6,5},{7,4},{8,11},{9,10},{10,... | collective-permute-start | bytes 442376 | tf_op jit(solution)/shard_map/ppermute | solution.py:616
  28.7 8.9 %collective-permute-start.5 = (bf16[4,144,128]{2,1,0:T(8,128)(2,1)S(1)}, bf16[4,144,128]{2,1,0:T(8,128)(2,1)S(1)}, u32[]{:S(2)}, u32[]{:S(2)}) collective-permute-start(bf16[4,144,128]{2,1,0:T(8,128)(2,1)S(1)} %get-tuple-element.46.rest_0_), channel_id=1, source_target_pairs={{0,2},{1,3},{2,0},{3,1},{4,6},{5,7},{6,4},{7,5},{8,10},{9,11},{10,... | collective-permute-start | bytes 442376 | tf_op jit(solution)/shard_map/ppermute | solution.py:616
  28.7 9.0 %collective-permute-start.4 = (bf16[4,144,128]{2,1,0:T(8,128)(2,1)S(1)}, bf16[4,144,128]{2,1,0:T(8,128)(2,1)S(1)}, u32[]{:S(2)}, u32[]{:S(2)}) collective-permute-start(bf16[4,144,128]{2,1,0:T(8,128)(2,1)S(1)} %get-tuple-element.46.rest_0_), channel_id=1, source_target_pairs={{0,1},{1,0},{2,3},{3,2},{4,5},{5,4},{6,7},{7,6},{8,9},{9,8},{10,11... | collective-permute-start | bytes 442376 | tf_op jit(solution)/shard_map/ppermute | solution.py:616

commit v6 on v5

--- a/solution.py
+++ b/solution.py
@@ -13,7 +13,7 @@
 CHUNK = 16
 UNROLL = 16
 STEP = 16
-GROW = 16
+GROW = 8
 MIB = 1024 * 1024
 F32 = jnp.float32
 BF16 = jnp.bfloat16

time: 43.6 us -> 43.5 us (level)
  no operation moved by 1% of the time
where the time goes in v6:
time: 43.5 us; the launch traced here: 43 us
  Pallas kernels  22.6 us (52%)
  starting transfers between devices  16.5 us (38%)
  waiting for transfers between devices  3.67 us (8%)
    pallas_call x1, Pallas kernels, local(): pl.pallas_call(bulk_kernel, out_shape=sds(density.shape, F32), in_specs=[...  8.48 us
    all_to_all x1, starting transfers between devices, local(): lax.all_to_all(sent, 'tile', split_axis=0, concat_axis=0, tiled=True)  7.03 us
    ppermute x1, starting transfers between devices, local(): got_b = lax.ppermute(cols_b, 'flow', far_pairs(flows))  4.47 us
    pallas_call x1, Pallas kernels, local(): pl.pallas_call(edges_kernel, out_shape=(message, message, message, messag...  3.76 us
    pallas_call x1, Pallas kernels, local(): pl.pallas_call(land_kernel, out_shape=sds(density.shape, F32), in_specs=[...  3.61 us
    pallas_call x1, Pallas kernels, local(): pl.pallas_call(grow_kernel, out_shape=pltpu.HBM(density.shape, F32), in_s...  3.15 us
    pallas_call x1, Pallas kernels, local(): pl.pallas_call(hubs_kernel, out_shape=(sds((bands * stride, cols), BF16),...  2.92 us
    ppermute x3, starting transfers between devices, swap(): return lax.ppermute(x, 'flow', [(i, i ^ bit) for i in range(flows)])  2.36 us
  transfers between devices with their start and end apart: 8, of which 2 were waited for; matrix products, arithmetic and copies ran while one was open for 0% of the time, Pallas kernels for 27%

profile of v6, /device:TPU:1, one launch (start us, length us, event | category | flops | bytes accessed | tf_op | source)
XLA Modules:
  0.0 43.0 jit_solution(11104902285781874775)
XLA Ops:
  0.0 0.1 pad_add_fusion.place
  0.1 3.8 %edges.1 = (bf16[144,128]{1,0:T(8,128)(2,1)S(1)}, bf16[144,128]{1,0:T(8,128)(2,1)S(1)}, bf16[144,128]{1,0:T(8,128)(2,1)S(1)}, bf16[144,128]{1,0:T(8,128)(2,1)S(1...) custom-call(s32[4]{0:T(128)S(1)} %pad_add_fusion.place, ...), custom_call_target="tpu_custom_call" | custom-call | tf_op jit(solution)/shard_map/edges/pallas_call | solution.py:582
  3.8 0.0 copy-start
  3.9 0.0 copy-start.1
  3.9 0.0 copy-start.2
  3.9 0.0 copy-start.3
  3.9 0.0 copy-start.4
  3.9 0.1 collective-permute-start
  4.0 4.5 %collective-permute-start.1 = (bf16[144,128]{1,0:T(8,128)(2,1)S(1)}, bf16[144,128]{1,0:T(8,128)(2,1)S(1)}, u32[]{:S(2)}, u32[]{:S(2)}) collective-permute-start(bf16[144,128]{1,0:T(8,128)(2,1)S(1)} %get-tuple-element.30), channel_id=1, source_target_pairs={{1,2},{2,1},{5,6},{6,5},{9,10},{10,9},{13,14},{14,13},{17,18},{18,... | collective-permute-start | bytes 110600 | tf_op jit(solution)/shard_map/ppermute | solution.py:602
  8.5 0.0 collective-permute-done.got_a.cols_a
  8.5 1.9 %collective-permute-done.1.got_b.cols_b = bf16[144,128]{1,0:T(8,128)(2,1)S(1)} collective-permute-done((bf16[144,128]{1,0:T(8,128)(2,1)S(1)}, bf16[144,128]{1,0:T(8,128)(2,1)S(1)}, u32[]{:S(2)}, u32[]{:S(2)}) %collective-permute-start.1) | collective-permute-done | bytes 36896 | tf_op jit(solution)/shard_map/ppermute | solution.py:602
  10.4 0.6 %corners.1 = (bf16[144,128]{1,0:T(8,128)(2,1)S(1)}, bf16[144,128]{1,0:T(8,128)(2,1)S(1)}) custom-call(s32[4]{0:T(128)S(1)} %pad_add_fusion.place, bf16[144,128]{1,0:T(8,128)(2,1)S(1)} %get-tuple-element.27.rows_a, bf16[144,128]{1,0:T(8,128)(2,1)S(1)} %get-tuple-element.28.rows_b, bf16[144,128]{1,0:T(8,128)(2,1)S(1)} %collective-permute-done.got_a.cols_a, ...), custom_call_target="tpu_custom_call" | custom-call | tf_op jit(solution)/shard_map/corners/pallas_call | solution.py:603
  11.1 1.9 %collective-permute-start.2 = (bf16[144,128]{1,0:T(8,128)(2,1)S(1)}, bf16[144,128]{1,0:T(8,128)(2,1)S(1)}, u32[]{:S(2)}, u32[]{:S(2)}) collective-permute-start(bf16[144,128]{1,0:T(8,128)(2,1)S(1)} %get-tuple-element.37), channel_id=1, source_target_pairs={{0,4},{4,0},{8,12},{12,8},{16,20},{20,16},{24,28},{28,24},{1,5},{5... | collective-permute-start | bytes 110600 | tf_op jit(solution)/shard_map/ppermute | solution.py:612
  12.9 0.7 %collective-permute-start.3 = (bf16[144,128]{1,0:T(8,128)(2,1)S(1)}, bf16[144,128]{1,0:T(8,128)(2,1)S(1)}, u32[]{:S(2)}, u32[]{:S(2)}) collective-permute-start(bf16[144,128]{1,0:T(8,128)(2,1)S(1)} %get-tuple-element.38), channel_id=1, source_target_pairs={{4,8},{8,4},{12,16},{16,12},{20,24},{24,20},{5,9},{9,5},{13,17},{1... | collective-permute-start | bytes 110600 | tf_op jit(solution)/shard_map/ppermute | solution.py:613
  13.6 3.2 %grow.1 = f32[64,128,128]{2,1,0:T(8,128)} custom-call(bf16[64,128,128]{2,1,0:T(8,128)(2,1)} %draw, f32[128,128]{1,0:T(8,128)} %threshold.1), custom_call_target="tpu_custom_call" | custom-call | tf_op jit(solution)/shard_map/grow/pallas_call | solution.py:618
  16.8 2.9 %hubs.1 = (bf16[2176,128]{1,0:T(8,128)(2,1)}, f32[128,128]{1,0:T(8,128)S(1)}, f32[128,128]{1,0:T(8,128)S(1)}, f32[256,128]{1,0:T(8,128)S(1)}, f32[144,128]{1,0:T(8,128)S(1)}, /*index=5*/f32[4,64,128]{2,1,0:T(8,128)S(1)}) custom-call(s32[4]{0:T(128)S(1)} %pad_add_fusion.place, s32[16]{0:T(128)S(1)} %bitcast.13, s32[16]{0:T(128)S(1)} %bitcast.17, ...), custom_call_target="tpu_custom_call" | custom-call | tf_op jit(solution)/shard_map/hubs/pallas_call | solution.py:640
  19.7 7.0 %all-to-all-start = ((bf16[8,272,128]{2,1,0:T(8,128)(2,1)}), bf16[8,272,128]{2,1,0:T(8,128)(2,1)S(1)}, u32[]{:S(2)}, u32[]{:S(2)}) async-start(bf16[8,272,128]{2,1,0:T(8,128)(2,1)} %bitcast.10), calls=%async_computation | async-start | bytes 1114112 | tf_op jit(solution)/shard_map/all_to_all | solution.py:652
  26.8 1.9 %collective-permute-start.6 = (bf16[4,144,128]{2,1,0:T(8,128)(2,1)S(1)}, bf16[4,144,128]{2,1,0:T(8,128)(2,1)S(1)}, u32[]{:S(2)}, u32[]{:S(2)}) collective-permute-start(bf16[4,144,128]{2,1,0:T(8,128)(2,1)S(1)} %get-tuple-element.46.rest_0_), channel_id=1, source_target_pairs={{0,3},{1,2},{2,1},{3,0},{4,7},{5,6},{6,5},{7,4},{8,11},{9,10},{10,... | collective-permute-start | bytes 442376 | tf_op jit(solution)/shard_map/ppermute | solution.py:616
  28.7 0.0 collective-permute-start.5
  28.7 0.5 %collective-permute-start.4 = (bf16[4,144,128]{2,1,0:T(8,128)(2,1)S(1)}, bf16[4,144,128]{2,1,0:T(8,128)(2,1)S(1)}, u32[]{:S(2)}, u32[]{:S(2)}) collective-permute-start(bf16[4,144,128]{2,1,0:T(8,128)(2,1)S(1)} %get-tuple-element.46.rest_0_), channel_id=1, source_target_pairs={{0,1},{1,0},{2,3},{3,2},{4,5},{5,4},{6,7},{7,6},{8,9},{9,8},{10,11... | collective-permute-start | bytes 442376 | tf_op jit(solution)/shard_map/ppermute | solution.py:616
  29.1 8.5 %bulk.1.kept = f32[64,128,128]{2,1,0:T(8,128)} custom-call(s32[16]{0:T(128)S(1)} %bitcast.14, f32[16]{0:T(128)S(1)} %bitcast.16, f32[64,128,128]{2,1,0:T(8,128)} %density.3, f32[64,128,128]{2,1,0:T(8,128)} %grow.1, f32[144,128]{1,0:T(8,128)S(1)} %get-tuple-element.41.coef, f32[4,64,128]{2,1,0:T(8,128)S(1)} %get-tuple-element.42.strips, ...), custom_call_target="tpu_custom_call" | custom-call | tf_op jit(solution)/shard_map/bulk/pallas_call | solution.py:653
  37.7 0.0 collective-permute-done.4.rest_1_
  37.7 1.7 %all-to-all-done = bf16[8,272,128]{2,1,0:T(8,128)(2,1)S(1)} async-done(((bf16[8,272,128]{2,1,0:T(8,128)(2,1)}), bf16[8,272,128]{2,1,0:T(8,128)(2,1)S(1)}, u32[]{:S(2)}, u32[]{:S(2)}) %all-to-all-start) | async-done | bytes 557088 | tf_op jit(solution)/shard_map/all_to_all | solution.py:652
  39.4 3.6 %land.1 = f32[64,128,128]{2,1,0:T(8,128)} custom-call(s32[4]{0:T(128)S(1)} %pad_add_fusion.place, bf16[2176,128]{1,0:T(8,128)(2,1)S(1)} %bitcast.12, f32[64,128,128]{2,1,0:T(8,128)} %bulk.1.kept, f32[64,128,128]{2,1,0:T(8,128)} %grow.1, bf16[4,144,128]{2,1,0:T(8,128)(2,1)S(1)} %get-tuple-element.46.rest_0_, ...), custom_call_target="tpu_custom_call", output_to_operand_aliasing={{}: (2, {})} | custom-call | tf_op jit(solution)/shard_map/land/pallas_call | solution.py:672
  (9 shorter events, 0.0 us)
Async XLA Ops:
  3.8 12.9 %copy-start = (s32[1,16]{1,0:T(1,128)S(1)}, s32[1,16]{1,0:T(1,128)}, u32[]{:S(2)}) copy-start(s32[1,16]{1,0:T(1,128)} %param.17) | copy-start | bytes 196
  3.9 12.9 %copy-start.1 = (f32[1,16]{1,0:T(1,128)S(1)}, f32[1,16]{1,0:T(1,128)}, u32[]{:S(2)}) copy-start(f32[1,16]{1,0:T(1,128)} %param.21) | copy-start | bytes 196
  3.9 12.9 %copy-start.2 = (s32[1,16,1]{1,2,0:T(1,128)S(1)}, s32[1,16,1]{1,2,0:T(1,128)}, u32[]{:S(2)}) copy-start(s32[1,16,1]{1,2,0:T(1,128)} %param.18) | copy-start | bytes 196
  3.9 12.9 %copy-start.3 = (s32[1,16]{1,0:T(1,128)S(1)}, s32[1,16]{1,0:T(1,128)}, u32[]{:S(2)}) copy-start(s32[1,16]{1,0:T(1,128)} %param.19) | copy-start | bytes 196
  3.9 12.9 %copy-start.4 = (s32[1,16]{1,0:T(1,128)S(1)}, s32[1,16]{1,0:T(1,128)}, u32[]{:S(2)}) copy-start(s32[1,16]{1,0:T(1,128)} %param.20) | copy-start | bytes 196
  3.9 4.6 %collective-permute-start = (bf16[144,128]{1,0:T(8,128)(2,1)S(1)}, bf16[144,128]{1,0:T(8,128)(2,1)S(1)}, u32[]{:S(2)}, u32[]{:S(2)}) collective-permute-start(bf16[144,128]{1,0:T(8,128)(2,1)S(1)} %get-tuple-element.29), channel_id=1, source_target_pairs={{0,1},{1,0},{2,3},{3,2},{4,5},{5,4},{6,7},{7,6},{8,9},{9,8},{10,11... | collective-permute-start | bytes 110600 | tf_op jit(solution)/shard_map/ppermute | solution.py:601
  4.0 6.4 %collective-permute-start.1 = (bf16[144,128]{1,0:T(8,128)(2,1)S(1)}, bf16[144,128]{1,0:T(8,128)(2,1)S(1)}, u32[]{:S(2)}, u32[]{:S(2)}) collective-permute-start(bf16[144,128]{1,0:T(8,128)(2,1)S(1)} %get-tuple-element.30), channel_id=1, source_target_pairs={{1,2},{2,1},{5,6},{6,5},{9,10},{10,9},{13,14},{14,13},{17,18},{18,... | collective-permute-start | bytes 110600 | tf_op jit(solution)/shard_map/ppermute | solution.py:602
  11.1 5.7 %collective-permute-start.2 = (bf16[144,128]{1,0:T(8,128)(2,1)S(1)}, bf16[144,128]{1,0:T(8,128)(2,1)S(1)}, u32[]{:S(2)}, u32[]{:S(2)}) collective-permute-start(bf16[144,128]{1,0:T(8,128)(2,1)S(1)} %get-tuple-element.37), channel_id=1, source_target_pairs={{0,4},{4,0},{8,12},{12,8},{16,20},{20,16},{24,28},{28,24},{1,5},{5... | collective-permute-start | bytes 110600 | tf_op jit(solution)/shard_map/ppermute | solution.py:612
  12.9 3.8 %collective-permute-start.3 = (bf16[144,128]{1,0:T(8,128)(2,1)S(1)}, bf16[144,128]{1,0:T(8,128)(2,1)S(1)}, u32[]{:S(2)}, u32[]{:S(2)}) collective-permute-start(bf16[144,128]{1,0:T(8,128)(2,1)S(1)} %get-tuple-element.38), channel_id=1, source_target_pairs={{4,8},{8,4},{12,16},{16,12},{20,24},{24,20},{5,9},{9,5},{13,17},{1... | collective-permute-start | bytes 110600 | tf_op jit(solution)/shard_map/ppermute | solution.py:613
  19.7 19.7 %all-to-all-start = ((bf16[8,272,128]{2,1,0:T(8,128)(2,1)}), bf16[8,272,128]{2,1,0:T(8,128)(2,1)S(1)}, u32[]{:S(2)}, u32[]{:S(2)}) async-start(bf16[8,272,128]{2,1,0:T(8,128)(2,1)} %bitcast.10), calls=%async_computation | async-start | bytes 1114112 | tf_op jit(solution)/shard_map/all_to_all | solution.py:652
  26.8 10.9 %collective-permute-start.6 = (bf16[4,144,128]{2,1,0:T(8,128)(2,1)S(1)}, bf16[4,144,128]{2,1,0:T(8,128)(2,1)S(1)}, u32[]{:S(2)}, u32[]{:S(2)}) collective-permute-start(bf16[4,144,128]{2,1,0:T(8,128)(2,1)S(1)} %get-tuple-element.46.rest_0_), channel_id=1, source_target_pairs={{0,3},{1,2},{2,1},{3,0},{4,7},{5,6},{6,5},{7,4},{8,11},{9,10},{10,... | collective-permute-start | bytes 442376 | tf_op jit(solution)/shard_map/ppermute | solution.py:616
  28.7 9.0 %collective-permute-start.5 = (bf16[4,144,128]{2,1,0:T(8,128)(2,1)S(1)}, bf16[4,144,128]{2,1,0:T(8,128)(2,1)S(1)}, u32[]{:S(2)}, u32[]{:S(2)}) collective-permute-start(bf16[4,144,128]{2,1,0:T(8,128)(2,1)S(1)} %get-tuple-element.46.rest_0_), channel_id=1, source_target_pairs={{0,2},{1,3},{2,0},{3,1},{4,6},{5,7},{6,4},{7,5},{8,10},{9,11},{10,... | collective-permute-start | bytes 442376 | tf_op jit(solution)/shard_map/ppermute | solution.py:616
  28.7 9.0 %collective-permute-start.4 = (bf16[4,144,128]{2,1,0:T(8,128)(2,1)S(1)}, bf16[4,144,128]{2,1,0:T(8,128)(2,1)S(1)}, u32[]{:S(2)}, u32[]{:S(2)}) collective-permute-start(bf16[4,144,128]{2,1,0:T(8,128)(2,1)S(1)} %get-tuple-element.46.rest_0_), channel_id=1, source_target_pairs={{0,1},{1,0},{2,3},{3,2},{4,5},{5,4},{6,7},{7,6},{8,9},{9,8},{10,11... | collective-permute-start | bytes 442376 | tf_op jit(solution)/shard_map/ppermute | solution.py:616
